TPU v7x, 128 devices: a whole 4x4x4 slice. The times are simulated.
128 devices in a mesh: ty: 16 (over y, z_lo, core), tx: 8 (over z_hi, x).
Axes of the slice: x: 4, y: 4, z: 4 (z_hi: 2, z_lo: 2; z = z_hi * 2 + z_lo), core: 2. Of those that a mesh axis runs over, the one named last changes fastest.
Arguments:
- residual: float32 [128, 4, 128, 768], P(('ty', 'tx')), may hold values from -6 to 6
- counts: int32 [128, 128], P(('ty', 'tx')), may hold values from 96 to 768, as said below
- offsets: int32 [128, 2, 128, 768], P(('ty', 'tx')), may hold values from 2 to 122
- positions: float32 [128, 2, 128, 768], P(('ty', 'tx')), may hold values from 0 to 1
- coef_fine: float32 [4, 2048, 1024], P(None, 'ty', 'tx'), may hold values from -0.4 to 0.4
- coef_coarse: float32 [4, 1024, 512], P(None, 'ty', 'tx'), may hold values from -0.4 to 0.4
- kappa_map: int32 [2048, 1024], P('ty', 'tx'), may hold values from 0 to 7
- kappa_table: float32 [2, 8], replicated, may hold values from 0.05 to 3
- level_weight: float32 [2], replicated, may hold values from 0.5 to 2
Outputs:
- fine_grad: float32 [4, 2048, 1024], P(None, 'ty', 'tx')
- coarse_grad: float32 [4, 1024, 512], P(None, 'ty', 'tx')
Inputs may be any that keep to these rules, and one draw needn't show every extreme that they name: counts[s, d] is the number of live leading rows in the bin from tile s to tile d; in every draw some destination tiles receive 768 live rows from every source. offsets keep every row's 4 x 4 fine patch and 4 x 4 coarse patch inside its destination tile.
All inputs are finite; a program needn't handle non-finite values.
Results may differ from a plain program's by a relative error of at most 0.0032.
Values sent between devices are 32-bit elements; how exact they have to be, the bound alone decides.
No kernel may reach another device: no remote copies, remote signals or barrier semaphores. Data moves between devices by JAX's collectives and lax.ppermute only.
A program may use at most 64 MiB of HBM per device.

v0:
```python
import jax
import jax.numpy as jnp
from jax import lax
from jax.sharding import PartitionSpec as P


def with_halo(shard, sides, width):
    for axis, dim in sides:
        count, length = (lax.axis_size(axis), shard.shape[dim])
        up = [(i, (i + 1) % count) for i in range(count - 1)]
        down = [(j, i) for i, j in up]
        last = lax.slice_in_dim(shard, length - width, length, axis=dim)
        first = lax.slice_in_dim(shard, 0, width, axis=dim)
        before = lax.ppermute(last, axis, up)
        after = lax.ppermute(first, axis, down)
        shard = jnp.concatenate([before, shard, after], axis=dim)
    return shard


def spline(t):
    s = 1.0 - t
    return (
        s * s * s / 6.0,
        (3.0 * t * t * t - 6.0 * t * t + 4.0) / 6.0,
        (-3.0 * t * t * t + 3.0 * t * t + 3.0 * t + 1.0) / 6.0,
        t * t * t / 6.0,
    )


def project(values, cells, fracs, side):
    channels, tiles, slots = values.shape
    group = 1
    while group * 2 <= tiles and group * 2 * slots <= 16384:
        group = group * 2
    steps = tiles // group

    def add_block(step, total):
        first = step * group
        block_values = lax.dynamic_slice_in_dim(values, first, group, 1)
        block_cells = lax.dynamic_slice_in_dim(cells, first, group, 1)
        block_fracs = lax.dynamic_slice_in_dim(fracs, first, group, 1)
        lattice = lax.broadcasted_iota(jnp.int32, (side, group, slots), 0)
        weight_y = spline(block_fracs[0])
        weight_x = spline(block_fracs[1])
        column_y = jnp.zeros((side, group, slots), jnp.float32)
        column_x = jnp.zeros((side, group, slots), jnp.float32)
        for a in range(4):
            column_y = column_y + jnp.where(
                lattice == block_cells[0][None] - 1 + a, weight_y[a][None], 0.0
            )
            column_x = column_x + jnp.where(
                lattice == block_cells[1][None] - 1 + a, weight_x[a][None], 0.0
            )
        spread = block_values[:, None] * column_y[None]
        left = spread.astype(jnp.bfloat16).reshape(channels * side, group * slots)
        right = column_x.astype(jnp.bfloat16).reshape(side, group * slots)
        product = lax.dot_general(
            left, right, (((1,), (1,)), ((), ())), preferred_element_type=jnp.float32
        )
        return total + product

    start = jnp.zeros((channels * side, side), jnp.float32)
    total = lax.fori_loop(0, steps, add_block, start)
    return total.reshape(channels, side, side)


def lookup(classes, table_row):
    total = jnp.zeros(classes.shape, jnp.float32)
    for kind in range(table_row.shape[0]):
        total = total + jnp.where(classes == kind, table_row[kind], 0.0)
    return 4.0 + total


def inner_sum(padded):
    return padded[:, 2:, 1:-1] + padded[:, :-2, 1:-1] + padded[:, 1:-1, 2:] + padded[:, 1:-1, :-2]


def rim_once(field, fine):
    if fine:
        return with_halo(field, (("ty", 1), ("tx", 2)), 1)
    return with_halo(field, (("ty", 1), ("tx", 2)), 1)


def precision(field, diag, fine):
    first = diag * field - inner_sum(rim_once(field, fine))
    return diag * first - inner_sum(rim_once(first, fine))


def on_device(
    residual,
    counts,
    offsets,
    positions,
    coef_fine,
    coef_coarse,
    kappa_map,
    kappa_table,
    level_weight,
):
    channels = residual.shape[1]
    tiles = residual.shape[2]
    slots = residual.shape[3]
    live = lax.broadcasted_iota(jnp.int32, residual.shape, 3) < counts[:, None, :, None]
    masked = jnp.where(live, residual, 0.0)
    arrived = lax.all_to_all(masked, ("ty", "tx"), split_axis=2, concat_axis=2, tiled=True)
    arrived = arrived.reshape(channels, tiles, slots)
    cells = offsets[0]
    fracs = positions[0]
    side = coef_fine.shape[1]
    half = coef_coarse.shape[1]
    fine_proj = project(arrived, cells, fracs, side)
    coarse_cells = cells // 2
    coarse_fracs = ((cells % 2).astype(jnp.float32) + fracs) * 0.5
    coarse_proj = project(arrived, coarse_cells, coarse_fracs, half)
    diag_fine = lookup(kappa_map, kappa_table[0])
    diag_coarse = lookup(kappa_map[::2, ::2], kappa_table[1])
    fine_grad = level_weight[0] * fine_proj - precision(coef_fine, diag_fine, True)
    coarse_grad = level_weight[1] * coarse_proj - precision(coef_coarse, diag_coarse, False)
    return (fine_grad, coarse_grad)


def solution(mesh):
    return jax.shard_map(
        on_device,
        mesh=mesh,
        in_specs=(
            P(("ty", "tx"), None, None, None),
            P(("ty", "tx"), None),
            P(("ty", "tx"), None, None, None),
            P(("ty", "tx"), None, None, None),
            P(None, "ty", "tx"),
            P(None, "ty", "tx"),
            P("ty", "tx"),
            P(),
            P(),
        ),
        out_specs=(P(None, "ty", "tx"), P(None, "ty", "tx")),
        check_vma=False,
    )
```

profile of v0, /device:TPU:39, one launch (start us, length us, event | category | flops | bytes accessed | tf_op | source)
XLA Modules:
  0.0 465.8 jit_solution(18075711496991175420)
XLA Ops:
  4.4 10.5 %all-to-all-start = ((f32[1,4,128,768]{3,1,0,2:T(4,128)}), f32[1,4,128,768]{3,1,0,2:T(4,128)S(1)}, u32[]{:S(2)}, u32[]{:S(2)}) async-start(f32[1,4,128,768]{3,1,0,2:T(4,128)} %copy_select_fusion), calls=%async_computation | async-start | bytes 3145728 | tf_op jit(solution)/shard_map/all_to_all | solution.py:105
  34.4 5.1 %add_add_fusion = f32[128,128]{1,0:T(8,128)S(1)} fusion(s32[128,128]{1,0:T(8,128)S(1)} %copy-done.10, f32[]{:T(128)} %bitcast.13, f32[]{:T(128)} %bitcast.12, f32[]{:T(128)} %bitcast.11, f32[]{:T(128)} %bitcast.10, f32[]{:T(128)} %bitcast.9, f32[]{:T(128)} %bitcast.8, f32[]{:T(128)} %bitcast.7, f32[]{:T(128)} %bitcast.6), kind=kLoop, calls=%fused_computation.186 | loop fusion | flops 393216 | bytes 131104 | tf_op jit(solution)/shard_map/add | solution.py:71
  39.5 5.2 %add_add_fusion.1 = f32[64,64]{1,0:T(8,128)S(1)} fusion(s32[64,64]{1,0:T(8,128)S(1)} %slice.353, f32[]{:T(128)} %bitcast.23, f32[]{:T(128)} %bitcast.22, f32[]{:T(128)} %bitcast.21, f32[]{:T(128)} %bitcast.20, f32[]{:T(128)} %bitcast.19, f32[]{:T(128)} %bitcast.18, f32[]{:T(128)} %bitcast.17, f32[]{:T(128)} %bitcast.16), kind=kLoop, calls=%fused_computation.187 | loop fusion | flops 98304 | bytes 32800 | tf_op jit(solution)/shard_map/add | solution.py:71
  51.8 7.6 %collective-permute-done.10 = f32[4,66,1]{2,1,0:T(8,128)S(1)} collective-permute-done((f32[4,66,1]{2,1,0:T(8,128)S(1)}, f32[4,66,1]{2,1,0:T(8,128)S(1)}, u32[]{:S(2)}, u32[]{:S(2)}) %collective-permute-start.10) | collective-permute-done | bytes 1088 | tf_op jit(solution)/shard_map/ppermute | solution.py:15
  75.2 5.3 %collective-permute-done.2 = f32[4,130,1]{2,1,0:T(8,128)S(1)} collective-permute-done((f32[4,130,1]{2,1,0:T(8,128)S(1)}, f32[4,130,1]{2,1,0:T(8,128)S(1)}, u32[]{:S(2)}, u32[]{:S(2)}) %collective-permute-start.2) | collective-permute-done | bytes 2112 | tf_op jit(solution)/shard_map/ppermute | solution.py:15
  94.3 5.5 %collective-permute-start.7 = (f32[4,130,1]{2,1,0:T(8,128)}, f32[4,130,1]{2,1,0:T(8,128)}, u32[]{:S(2)}, u32[]{:S(2)}) collective-permute-start(f32[4,130,1]{2,1,0:T(8,128)} %get-tuple-element.507), channel_id=1, source_target_pairs={{0,1},{1,2},{2,3},{3,4},{4,5},{5,6},{6,7},{8,9},{9,10},{10,11},{11... | collective-permute-start | bytes 6248 | tf_op jit(solution)/shard_map/ppermute | solution.py:14
  103.4 219.1 %while.38 = (s32[]{:T(128)}, f32[512,128]{1,0:T(8,128)S(1)}, f32[4,128,768]{2,1,0:T(8,128)}, s32[2,128,768]{2,1,0:T(8,128)}, f32[2,128,768]{2,1,0:T(8,128)}, /*i...) while((s32[]{:T(128)}, f32[512,128]{1,0:T(8,128)S(1)}, f32[4,128,768]{2,1,0:T(8,128)}, ...), condition=%wide.region_1.2_spmd.clone, body=%wide.region_0.1_spmd.clone.sunk | while | flops 1660116992 | bytes 78381248 | solution.py:63
  114.2 8.9 %copy.25 = bf16[64,8,16,768]{3,1,2,0:T(8,128)(2,1)} copy(bf16[64,8,16,768]{3,2,1,0:T(8,128)(2,1)S(1)} %bitcast.137) | data formatting | bytes 25165824 | tf_op jit(solution)/shard_map/while
  124.4 6.4 %convolution_add_fusion.4 = f32[512,128]{1,0:T(8,128)S(1)} fusion(bf16[512,12288]{1,0:T(8,128)(2,1)} %bitcast.140, bf16[128,12288]{1,0:T(8,128)(2,1)S(1)} %bitcast.144, f32[512,128]{1,0:T(8,128)S(1)} %get-tuple-element.685, pred[]{:T(512)S(6)} %compare.9), kind=kOutput, calls=%fused_computation.11.clone.1 | convolution fusion | flops 1610743808 | bytes 16252929 | tf_op jit(solution)/shard_map/while/body/eval_jaxpr/dot_general | solution.py:57
  141.6 8.9 %copy.25 = bf16[64,8,16,768]{3,1,2,0:T(8,128)(2,1)} copy(bf16[64,8,16,768]{3,2,1,0:T(8,128)(2,1)S(1)} %bitcast.137) | data formatting | bytes 25165824 | tf_op jit(solution)/shard_map/while
  151.7 6.4 %convolution_add_fusion.4 = f32[512,128]{1,0:T(8,128)S(1)} fusion(bf16[512,12288]{1,0:T(8,128)(2,1)} %bitcast.140, bf16[128,12288]{1,0:T(8,128)(2,1)S(1)} %bitcast.144, f32[512,128]{1,0:T(8,128)S(1)} %get-tuple-element.685, pred[]{:T(512)S(6)} %compare.9), kind=kOutput, calls=%fused_computation.11.clone.1 | convolution fusion | flops 1610743808 | bytes 16252929 | tf_op jit(solution)/shard_map/while/body/eval_jaxpr/dot_general | solution.py:57
  169.0 8.9 %copy.25 = bf16[64,8,16,768]{3,1,2,0:T(8,128)(2,1)} copy(bf16[64,8,16,768]{3,2,1,0:T(8,128)(2,1)S(1)} %bitcast.137) | data formatting | bytes 25165824 | tf_op jit(solution)/shard_map/while
  179.1 6.4 %convolution_add_fusion.4 = f32[512,128]{1,0:T(8,128)S(1)} fusion(bf16[512,12288]{1,0:T(8,128)(2,1)} %bitcast.140, bf16[128,12288]{1,0:T(8,128)(2,1)S(1)} %bitcast.144, f32[512,128]{1,0:T(8,128)S(1)} %get-tuple-element.685, pred[]{:T(512)S(6)} %compare.9), kind=kOutput, calls=%fused_computation.11.clone.1 | convolution fusion | flops 1610743808 | bytes 16252929 | tf_op jit(solution)/shard_map/while/body/eval_jaxpr/dot_general | solution.py:57
  196.4 8.9 %copy.25 = bf16[64,8,16,768]{3,1,2,0:T(8,128)(2,1)} copy(bf16[64,8,16,768]{3,2,1,0:T(8,128)(2,1)S(1)} %bitcast.137) | data formatting | bytes 25165824 | tf_op jit(solution)/shard_map/while
  206.5 6.4 %convolution_add_fusion.4 = f32[512,128]{1,0:T(8,128)S(1)} fusion(bf16[512,12288]{1,0:T(8,128)(2,1)} %bitcast.140, bf16[128,12288]{1,0:T(8,128)(2,1)S(1)} %bitcast.144, f32[512,128]{1,0:T(8,128)S(1)} %get-tuple-element.685, pred[]{:T(512)S(6)} %compare.9), kind=kOutput, calls=%fused_computation.11.clone.1 | convolution fusion | flops 1610743808 | bytes 16252929 | tf_op jit(solution)/shard_map/while/body/eval_jaxpr/dot_general | solution.py:57
  223.7 8.9 %copy.25 = bf16[64,8,16,768]{3,1,2,0:T(8,128)(2,1)} copy(bf16[64,8,16,768]{3,2,1,0:T(8,128)(2,1)S(1)} %bitcast.137) | data formatting | bytes 25165824 | tf_op jit(solution)/shard_map/while
  233.9 6.4 %convolution_add_fusion.4 = f32[512,128]{1,0:T(8,128)S(1)} fusion(bf16[512,12288]{1,0:T(8,128)(2,1)} %bitcast.140, bf16[128,12288]{1,0:T(8,128)(2,1)S(1)} %bitcast.144, f32[512,128]{1,0:T(8,128)S(1)} %get-tuple-element.685, pred[]{:T(512)S(6)} %compare.9), kind=kOutput, calls=%fused_computation.11.clone.1 | convolution fusion | flops 1610743808 | bytes 16252929 | tf_op jit(solution)/shard_map/while/body/eval_jaxpr/dot_general | solution.py:57
  251.1 8.9 %copy.25 = bf16[64,8,16,768]{3,1,2,0:T(8,128)(2,1)} copy(bf16[64,8,16,768]{3,2,1,0:T(8,128)(2,1)S(1)} %bitcast.137) | data formatting | bytes 25165824 | tf_op jit(solution)/shard_map/while
  261.3 6.4 %convolution_add_fusion.4 = f32[512,128]{1,0:T(8,128)S(1)} fusion(bf16[512,12288]{1,0:T(8,128)(2,1)} %bitcast.140, bf16[128,12288]{1,0:T(8,128)(2,1)S(1)} %bitcast.144, f32[512,128]{1,0:T(8,128)S(1)} %get-tuple-element.685, pred[]{:T(512)S(6)} %compare.9), kind=kOutput, calls=%fused_computation.11.clone.1 | convolution fusion | flops 1610743808 | bytes 16252929 | tf_op jit(solution)/shard_map/while/body/eval_jaxpr/dot_general | solution.py:57
  278.5 8.9 %copy.25 = bf16[64,8,16,768]{3,1,2,0:T(8,128)(2,1)} copy(bf16[64,8,16,768]{3,2,1,0:T(8,128)(2,1)S(1)} %bitcast.137) | data formatting | bytes 25165824 | tf_op jit(solution)/shard_map/while
  288.7 6.4 %convolution_add_fusion.4 = f32[512,128]{1,0:T(8,128)S(1)} fusion(bf16[512,12288]{1,0:T(8,128)(2,1)} %bitcast.140, bf16[128,12288]{1,0:T(8,128)(2,1)S(1)} %bitcast.144, f32[512,128]{1,0:T(8,128)S(1)} %get-tuple-element.685, pred[]{:T(512)S(6)} %compare.9), kind=kOutput, calls=%fused_computation.11.clone.1 | convolution fusion | flops 1610743808 | bytes 16252929 | tf_op jit(solution)/shard_map/while/body/eval_jaxpr/dot_general | solution.py:57
  305.9 8.9 %copy.25 = bf16[64,8,16,768]{3,1,2,0:T(8,128)(2,1)} copy(bf16[64,8,16,768]{3,2,1,0:T(8,128)(2,1)S(1)} %bitcast.137) | data formatting | bytes 25165824 | tf_op jit(solution)/shard_map/while
  316.1 6.4 %convolution_add_fusion.4 = f32[512,128]{1,0:T(8,128)S(1)} fusion(bf16[512,12288]{1,0:T(8,128)(2,1)} %bitcast.140, bf16[128,12288]{1,0:T(8,128)(2,1)S(1)} %bitcast.144, f32[512,128]{1,0:T(8,128)S(1)} %get-tuple-element.685, pred[]{:T(512)S(6)} %compare.9), kind=kOutput, calls=%fused_computation.11.clone.1 | convolution fusion | flops 1610743808 | bytes 16252929 | tf_op jit(solution)/shard_map/while/body/eval_jaxpr/dot_general | solution.py:57
  322.6 137.8 %while.39 = (s32[]{:T(128)}, f32[256,64]{0,1:T(8,128)S(1)}, f32[4,128,768]{2,1,0:T(8,128)}, s32[2,128,768]{2,1,0:T(8,128)}, f32[2,128,768]{2,1,0:T(8,128)}, /*in...) while((s32[]{:T(128)}, f32[256,64]{0,1:T(8,128)S(1)}, f32[4,128,768]{2,1,0:T(8,128)}, ...), condition=%wide.region_3.4_spmd.clone, body=%wide.region_2.3_spmd.clone.sunk | while | flops 427679744 | bytes 40239300 | solution.py:63
  329.2 5.4 %copy.27 = bf16[32,8,16,768]{3,1,2,0:T(8,128)(2,1)} copy(bf16[32,8,16,768]{3,2,1,0:T(8,128)(2,1)S(1)} %bitcast.138) | data formatting | bytes 12582912 | tf_op jit(solution)/shard_map/while
  346.4 5.4 %copy.27 = bf16[32,8,16,768]{3,1,2,0:T(8,128)(2,1)} copy(bf16[32,8,16,768]{3,2,1,0:T(8,128)(2,1)S(1)} %bitcast.138) | data formatting | bytes 12582912 | tf_op jit(solution)/shard_map/while
  363.6 5.4 %copy.27 = bf16[32,8,16,768]{3,1,2,0:T(8,128)(2,1)} copy(bf16[32,8,16,768]{3,2,1,0:T(8,128)(2,1)S(1)} %bitcast.138) | data formatting | bytes 12582912 | tf_op jit(solution)/shard_map/while
  380.8 5.4 %copy.27 = bf16[32,8,16,768]{3,1,2,0:T(8,128)(2,1)} copy(bf16[32,8,16,768]{3,2,1,0:T(8,128)(2,1)S(1)} %bitcast.138) | data formatting | bytes 12582912 | tf_op jit(solution)/shard_map/while
  398.0 5.4 %copy.27 = bf16[32,8,16,768]{3,1,2,0:T(8,128)(2,1)} copy(bf16[32,8,16,768]{3,2,1,0:T(8,128)(2,1)S(1)} %bitcast.138) | data formatting | bytes 12582912 | tf_op jit(solution)/shard_map/while
  415.2 5.4 %copy.27 = bf16[32,8,16,768]{3,1,2,0:T(8,128)(2,1)} copy(bf16[32,8,16,768]{3,2,1,0:T(8,128)(2,1)S(1)} %bitcast.138) | data formatting | bytes 12582912 | tf_op jit(solution)/shard_map/while
  432.4 5.4 %copy.27 = bf16[32,8,16,768]{3,1,2,0:T(8,128)(2,1)} copy(bf16[32,8,16,768]{3,2,1,0:T(8,128)(2,1)S(1)} %bitcast.138) | data formatting | bytes 12582912 | tf_op jit(solution)/shard_map/while
  449.6 5.4 %copy.27 = bf16[32,8,16,768]{3,1,2,0:T(8,128)(2,1)} copy(bf16[32,8,16,768]{3,2,1,0:T(8,128)(2,1)S(1)} %bitcast.138) | data formatting | bytes 12582912 | tf_op jit(solution)/shard_map/while
  (204 shorter events, 257.7 us)
Async XLA Ops:
  0.7 27.3 %copy-start.11 = (f32[2,8]{1,0:T(2,128)S(1)}, f32[2,8]{1,0:T(2,128)}, u32[]{:S(2)}) copy-start(f32[2,8]{1,0:T(2,128)} %param.20) | copy-start | bytes 196
  4.4 29.3 %copy-start.10 = (s32[128,128]{1,0:T(8,128)S(1)}, s32[128,128]{1,0:T(8,128)}, u32[]{:S(2)}) copy-start(s32[128,128]{1,0:T(8,128)} %param.19) | copy-start | bytes 196612
  4.4 40.3 %copy-start.20 = (f32[2]{0:T(128)S(1)}, f32[2]{0:T(128)}, u32[]{:S(2)}) copy-start(f32[2]{0:T(128)} %param.21) | copy-start | bytes 28
  4.4 97.5 %all-to-all-start = ((f32[1,4,128,768]{3,1,0,2:T(4,128)}), f32[1,4,128,768]{3,1,0,2:T(4,128)S(1)}, u32[]{:S(2)}, u32[]{:S(2)}) async-start(f32[1,4,128,768]{3,1,0,2:T(4,128)} %copy_select_fusion), calls=%async_computation | async-start | bytes 3145728 | tf_op jit(solution)/shard_map/all_to_all | solution.py:105
  14.9 36.7 %collective-permute-start = (f32[4,1,128]{2,1,0:T(1,128)S(1)}, f32[4,1,128]{2,1,0:T(1,128)S(1)}, u32[]{:S(2)}, u32[]{:S(2)}) collective-permute-start(f32[4,1,128]{2,1,0:T(1,128)S(1)} %get-tuple-element.513), channel_id=1, source_target_pairs={{8,0},{16,8},{24,16},{32,24},{40,32},{48,40},{56,48},{64,56},{72,6... | collective-permute-start | bytes 6152 | tf_op jit(solution)/shard_map/ppermute | solution.py:15
  17.2 34.5 %collective-permute-start.1 = (f32[4,1,128]{2,1,0:T(1,128)S(1)}, f32[4,1,128]{2,1,0:T(1,128)S(1)}, u32[]{:S(2)}, u32[]{:S(2)}) collective-permute-start(f32[4,1,128]{2,1,0:T(1,128)S(1)} %get-tuple-element.512), channel_id=1, source_target_pairs={{0,8},{8,16},{16,24},{24,32},{32,40},{40,48},{48,56},{56,64},{64,7... | collective-permute-start | bytes 6152 | tf_op jit(solution)/shard_map/ppermute | solution.py:14
  21.4 24.0 %collective-permute-start.8 = (f32[4,1,64]{2,1,0:T(1,128)S(1)}, f32[4,1,64]{2,1,0:T(1,128)S(1)}, u32[]{:S(2)}, u32[]{:S(2)}) collective-permute-start(f32[4,1,64]{2,1,0:T(1,128)S(1)} %get-tuple-element.521), channel_id=1, source_target_pairs={{8,0},{16,8},{24,16},{32,24},{40,32},{48,40},{56,48},{64,56},{72,6... | collective-permute-start | bytes 3080 | tf_op jit(solution)/shard_map/ppermute | solution.py:15
  23.4 22.0 %collective-permute-start.9 = (f32[4,1,64]{2,1,0:T(1,128)S(1)}, f32[4,1,64]{2,1,0:T(1,128)S(1)}, u32[]{:S(2)}, u32[]{:S(2)}) collective-permute-start(f32[4,1,64]{2,1,0:T(1,128)S(1)} %get-tuple-element.520), channel_id=1, source_target_pairs={{0,8},{8,16},{16,24},{24,32},{32,40},{40,48},{48,56},{56,64},{64,7... | collective-permute-start | bytes 3080 | tf_op jit(solution)/shard_map/ppermute | solution.py:14
  39.5 54.8 %copy-start.5 = (f32[128,128]{1,0:T(8,128)}, f32[128,128]{1,0:T(8,128)S(1)}, u32[]{:S(2)}) copy-start(f32[128,128]{1,0:T(8,128)S(1)} %add_add_fusion) | copy-start | bytes 196612
  44.7 49.6 %copy-start.8 = (f32[64,64]{1,0:T(8,128)}, f32[64,64]{1,0:T(8,128)S(1)}, u32[]{:S(2)}) copy-start(f32[64,64]{1,0:T(8,128)S(1)} %add_add_fusion.1) | copy-start | bytes 49156
  45.5 6.3 %collective-permute-start.11 = (f32[4,66,1]{2,1,0:T(8,128)S(1)}, f32[4,66,1]{2,1,0:T(8,128)S(1)}, u32[]{:S(2)}, u32[]{:S(2)}) collective-permute-start(f32[4,66,1]{2,1,0:T(8,128)S(1)} %get-tuple-element.517), channel_id=1, source_target_pairs={{0,1},{1,2},{2,3},{3,4},{4,5},{5,6},{6,7},{8,9},{9,10},{10,11},{11... | collective-permute-start | bytes 3176 | tf_op jit(solution)/shard_map/ppermute | solution.py:14
  49.7 9.7 %collective-permute-start.10 = (f32[4,66,1]{2,1,0:T(8,128)S(1)}, f32[4,66,1]{2,1,0:T(8,128)S(1)}, u32[]{:S(2)}, u32[]{:S(2)}) collective-permute-start(f32[4,66,1]{2,1,0:T(8,128)S(1)} %get-tuple-element.516), channel_id=1, source_target_pairs={{1,0},{2,1},{3,2},{4,3},{5,4},{6,5},{7,6},{9,8},{10,9},{11,10},{12... | collective-permute-start | bytes 3176 | tf_op jit(solution)/shard_map/ppermute | solution.py:15
  59.7 11.9 %collective-permute-start.12 = (f32[4,1,64]{2,1,0:T(1,128)S(1)}, f32[4,1,64]{2,1,0:T(1,128)S(1)}, u32[]{:S(2)}, u32[]{:S(2)}) collective-permute-start(f32[4,1,64]{2,1,0:T(1,128)S(1)} %get-tuple-element.519), channel_id=1, source_target_pairs={{8,0},{16,8},{24,16},{32,24},{40,32},{48,40},{56,48},{64,56},{72,6... | collective-permute-start | bytes 3080 | tf_op jit(solution)/shard_map/ppermute | solution.py:15
  61.6 10.0 %collective-permute-start.13 = (f32[4,1,64]{2,1,0:T(1,128)S(1)}, f32[4,1,64]{2,1,0:T(1,128)S(1)}, u32[]{:S(2)}, u32[]{:S(2)}) collective-permute-start(f32[4,1,64]{2,1,0:T(1,128)S(1)} %get-tuple-element.518), channel_id=1, source_target_pairs={{0,8},{8,16},{16,24},{24,32},{32,40},{40,48},{48,56},{56,64},{64,7... | collective-permute-start | bytes 3080 | tf_op jit(solution)/shard_map/ppermute | solution.py:14
  66.3 8.9 %collective-permute-start.3 = (f32[4,130,1]{2,1,0:T(8,128)S(1)}, f32[4,130,1]{2,1,0:T(8,128)S(1)}, u32[]{:S(2)}, u32[]{:S(2)}) collective-permute-start(f32[4,130,1]{2,1,0:T(8,128)S(1)} %get-tuple-element.509), channel_id=1, source_target_pairs={{0,1},{1,2},{2,3},{3,4},{4,5},{5,6},{6,7},{8,9},{9,10},{10,11},{11... | collective-permute-start | bytes 6248 | tf_op jit(solution)/shard_map/ppermute | solution.py:14
  68.2 12.2 %collective-permute-start.2 = (f32[4,130,1]{2,1,0:T(8,128)S(1)}, f32[4,130,1]{2,1,0:T(8,128)S(1)}, u32[]{:S(2)}, u32[]{:S(2)}) collective-permute-start(f32[4,130,1]{2,1,0:T(8,128)S(1)} %get-tuple-element.508), channel_id=1, source_target_pairs={{1,0},{2,1},{3,2},{4,3},{5,4},{6,5},{7,6},{9,8},{10,9},{11,10},{12... | collective-permute-start | bytes 6248 | tf_op jit(solution)/shard_map/ppermute | solution.py:15
  71.6 31.8 %copy-start.12 = (f32[4,1,64]{2,1,0:T(1,128)}, f32[4,1,64]{2,1,0:T(1,128)S(1)}, u32[]{:S(2)}) copy-start(f32[4,1,64]{2,1,0:T(1,128)S(1)} %collective-permute-done.12) | copy-start | bytes 3076
  71.6 31.8 %copy-start.14 = (f32[4,1,64]{2,1,0:T(1,128)}, f32[4,1,64]{2,1,0:T(1,128)S(1)}, u32[]{:S(2)}) copy-start(f32[4,1,64]{2,1,0:T(1,128)S(1)} %collective-permute-done.13) | copy-start | bytes 3076
  80.8 12.5 %collective-permute-start.4 = (f32[4,1,128]{2,1,0:T(1,128)S(1)}, f32[4,1,128]{2,1,0:T(1,128)S(1)}, u32[]{:S(2)}, u32[]{:S(2)}) collective-permute-start(f32[4,1,128]{2,1,0:T(1,128)S(1)} %get-tuple-element.511), channel_id=1, source_target_pairs={{8,0},{16,8},{24,16},{32,24},{40,32},{48,40},{56,48},{64,56},{72,6... | collective-permute-start | bytes 6152 | tf_op jit(solution)/shard_map/ppermute | solution.py:15
  82.7 10.6 %collective-permute-start.5 = (f32[4,1,128]{2,1,0:T(1,128)S(1)}, f32[4,1,128]{2,1,0:T(1,128)S(1)}, u32[]{:S(2)}, u32[]{:S(2)}) collective-permute-start(f32[4,1,128]{2,1,0:T(1,128)S(1)} %get-tuple-element.510), channel_id=1, source_target_pairs={{0,8},{8,16},{16,24},{24,32},{32,40},{40,48},{48,56},{56,64},{64,7... | collective-permute-start | bytes 6152 | tf_op jit(solution)/shard_map/ppermute | solution.py:14
  88.0 375.9 %collective-permute-start.15 = (f32[4,66,1]{2,1,0:T(8,128)}, f32[4,66,1]{2,1,0:T(8,128)}, u32[]{:S(2)}, u32[]{:S(2)}) collective-permute-start(f32[4,66,1]{2,1,0:T(8,128)} %get-tuple-element.515), channel_id=1, source_target_pairs={{0,1},{1,2},{2,3},{3,4},{4,5},{5,6},{6,7},{8,9},{9,10},{10,11},{11... | collective-permute-start | bytes 3176 | tf_op jit(solution)/shard_map/ppermute | solution.py:14
  90.0 374.0 %collective-permute-start.14 = (f32[4,66,1]{2,1,0:T(8,128)}, f32[4,66,1]{2,1,0:T(8,128)}, u32[]{:S(2)}, u32[]{:S(2)}) collective-permute-start(f32[4,66,1]{2,1,0:T(8,128)} %get-tuple-element.514), channel_id=1, source_target_pairs={{1,0},{2,1},{3,2},{4,3},{5,4},{6,5},{7,6},{9,8},{10,9},{11,10},{12... | collective-permute-start | bytes 3176 | tf_op jit(solution)/shard_map/ppermute | solution.py:15
  94.3 366.7 %collective-permute-start.7 = (f32[4,130,1]{2,1,0:T(8,128)}, f32[4,130,1]{2,1,0:T(8,128)}, u32[]{:S(2)}, u32[]{:S(2)}) collective-permute-start(f32[4,130,1]{2,1,0:T(8,128)} %get-tuple-element.507), channel_id=1, source_target_pairs={{0,1},{1,2},{2,3},{3,4},{4,5},{5,6},{6,7},{8,9},{9,10},{10,11},{11... | collective-permute-start | bytes 6248 | tf_op jit(solution)/shard_map/ppermute | solution.py:14
  99.8 361.2 %collective-permute-start.6 = (f32[4,130,1]{2,1,0:T(8,128)}, f32[4,130,1]{2,1,0:T(8,128)}, u32[]{:S(2)}, u32[]{:S(2)}) collective-permute-start(f32[4,130,1]{2,1,0:T(8,128)} %get-tuple-element.506), channel_id=1, source_target_pairs={{1,0},{2,1},{3,2},{4,3},{5,4},{6,5},{7,6},{9,8},{10,9},{11,10},{12... | collective-permute-start | bytes 6248 | tf_op jit(solution)/shard_map/ppermute | solution.py:15
  322.5 138.5 %copy-start.1 = (f32[4,128,128]{2,1,0:T(8,128)S(1)}, f32[4,128,128]{2,1,0:T(8,128)}, u32[]{:S(2)}) copy-start(f32[4,128,128]{2,1,0:T(8,128)} %copy-done) | copy-start | bytes 786436
  322.6 138.5 %copy-start.6 = (f32[128,128]{1,0:T(8,128)S(1)}, f32[128,128]{1,0:T(8,128)}, u32[]{:S(2)}) copy-start(f32[128,128]{1,0:T(8,128)} %copy-done.5) | copy-start | bytes 196612
  322.6 138.5 %copy-start.17 = (f32[4,1,128]{2,1,0:T(1,128)S(1)}, f32[4,1,128]{2,1,0:T(1,128)}, u32[]{:S(2)}) copy-start(f32[4,1,128]{2,1,0:T(1,128)} %copy-done.16) | copy-start | bytes 6148
  322.6 138.5 %copy-start.19 = (f32[4,1,128]{2,1,0:T(1,128)S(1)}, f32[4,1,128]{2,1,0:T(1,128)}, u32[]{:S(2)}) copy-start(f32[4,1,128]{2,1,0:T(1,128)} %copy-done.18) | copy-start | bytes 6148
  322.6 141.4 %copy-start.3 = (f32[4,64,64]{2,1,0:T(8,128)S(1)}, f32[4,64,64]{2,1,0:T(8,128)}, u32[]{:S(2)}) copy-start(f32[4,64,64]{2,1,0:T(8,128)} %copy-done.2) | copy-start | bytes 196612
  322.6 141.4 %copy-start.9 = (f32[64,64]{1,0:T(8,128)S(1)}, f32[64,64]{1,0:T(8,128)}, u32[]{:S(2)}) copy-start(f32[64,64]{1,0:T(8,128)} %copy-done.8) | copy-start | bytes 49156
  322.6 141.4 %copy-start.13 = (f32[4,1,64]{2,1,0:T(1,128)S(1)}, f32[4,1,64]{2,1,0:T(1,128)}, u32[]{:S(2)}) copy-start(f32[4,1,64]{2,1,0:T(1,128)} %copy-done.12) | copy-start | bytes 3076
  322.6 141.4 %copy-start.15 = (f32[4,1,64]{2,1,0:T(1,128)S(1)}, f32[4,1,64]{2,1,0:T(1,128)}, u32[]{:S(2)}) copy-start(f32[4,1,64]{2,1,0:T(1,128)} %copy-done.14) | copy-start | bytes 3076
  (6 other events, 89.8 us)
where the time goes:
time: 472 us; the launch traced here: 466 us
  local copies, waits for them, and re-layouts  150 us (32%)
  other arithmetic  146 us (31%)
  matrix products  90.1 us (19%)
  starting transfers between devices  60.6 us (13%)
  waiting for transfers between devices  16.6 us (4%)
    while x32, local copies, waits for them, and re-layouts  129 us
    dot_general x16, matrix products, add_block(): lax.dot_general(left, right, (((1,), (1,)), ((), ())), preferred_element_...  90.1 us
    convert_element_type x16, other arithmetic, add_block(): right = column_x.astype(jnp.bfloat16).reshape(side, group * slots)  55.3 us
    convert_element_type x16, other arithmetic, add_block(): left = spread.astype(jnp.bfloat16).reshape(channels * side, group * slots)  37.8 us
    ppermute x8, starting transfers between devices, with_halo(): before = lax.ppermute(last, axis, up)  31.4 us
    ppermute x8, starting transfers between devices, with_halo(): after = lax.ppermute(first, axis, down)  18.8 us
    dynamic_slice x16, local copies, waits for them, and re-layouts, add_block(): block_values = lax.dynamic_slice_in_dim(values, first, group, 1)  15.2 us
    broadcast_in_dim x16, other arithmetic, add_block(): jnp.where(lattice == block_cells[1][None] - 1 + a, weight_x[a][None], 0.0)  14.5 us
  transfers between devices with their start and end apart: 17, of which 4 were waited for; matrix products, arithmetic and copies ran while one was open for 82% of the time, Pallas kernels for 0%

commit v1 on v0

v1 whole, which is shorter than its diff:
```python
import functools

import jax
import jax.numpy as jnp
from jax import lax
from jax.experimental import pallas as pl
from jax.experimental.pallas import tpu as pltpu
from jax.sharding import PartitionSpec as P

BF = jnp.bfloat16
F = jnp.float32
VMEM_LIMIT = 48 * 1024 * 1024
AXES = ("ty", "tx")


def struct(*shape):
    return jax.ShapeDtypeStruct(shape, F)


def iota(shape, dim):
    return lax.broadcasted_iota(jnp.int32, shape, dim)


def mm(a, b, dims=((1,), (0,))):
    return lax.dot_general(a, b, (dims, ((), ())), preferred_element_type=F)


def split3(a):
    hi = a.astype(BF)
    a = a - hi.astype(F)
    mid = a.astype(BF)
    lo = (a - mid.astype(F)).astype(BF)
    return hi, mid, lo


def params():
    return pltpu.CompilerParams(vmem_limit_bytes=VMEM_LIMIT)


def pack_kernel(block, counts_ref, res_ref, out_ref):
    base = pl.program_id(0) * block
    chunks = res_ref.shape[2] // 128
    own = iota((block, 128), 0) + base == iota((block, 128), 1)
    live = jnp.sum(jnp.where(own, counts_ref[...], 0).astype(F), axis=1, keepdims=True).astype(jnp.int32)
    for d in range(0, block, 8):
        for kc in range(chunks):
            slot = iota((8, 128), 1) + 128 * kc
            keep = slot < live[d:d + 8]
            for m in range(4):
                row = (d * chunks + kc) * 4 + m
                value = jnp.where(keep, res_ref[m, d:d + 8, 128 * kc:128 * kc + 128], 0.0)
                out_ref[pl.ds(row, 8, stride=4 * chunks), :] = value


def pack(counts, residual):
    channels, tiles, slots = residual.shape
    block = 32
    rows = 4 * (slots // 128)
    return pl.pallas_call(
        functools.partial(pack_kernel, block),
        grid=(tiles // block,),
        in_specs=[
            pl.BlockSpec((1, tiles), lambda i: (0, 0)),
            pl.BlockSpec((channels, block, slots), lambda i: (0, i, 0)),
        ],
        out_specs=pl.BlockSpec((block * rows, 128), lambda i: (i, 0)),
        out_shape=struct(tiles * rows, 128),
        compiler_params=params(),
        name="pack_rows",
    )(counts, residual)


def classes_to_diag(kinds, table_ref, level):
    total = jnp.zeros(kinds.shape, F)
    for k in range(table_ref.shape[1]):
        total = jnp.where(kinds == k, table_ref[level, k], total)
    return 4.0 + total


def columns_kernel(table_ref, cf_ref, cc_ref, km_ref, left_ref, right_ref, df_ref, dc_ref, square):
    left_ref[...] = jnp.zeros_like(left_ref)
    right_ref[...] = jnp.zeros_like(right_ref)
    square[...] = jnp.zeros_like(square)
    df = classes_to_diag(km_ref[...], table_ref, 0)
    df_ref[...] = df
    even = km_ref[pl.ds(0, 64, stride=2), :].astype(F).astype(BF)
    pick = jnp.where(iota((128, 128), 0) == 2 * iota((128, 128), 1), 1.0, 0.0).astype(BF)
    dc = classes_to_diag(mm(even, pick).astype(jnp.int32), table_ref, 1)
    dc = jnp.where(iota((64, 128), 1) < 64, dc, 0.0)
    dc_ref[...] = dc

    def send(row, turned, size, width):
        left_ref[pl.ds(row, width), :] = turned[0:width]
        right_ref[pl.ds(row, width), :] = turned[size - width:size]

    for m in range(4):
        send(2 * m, cf_ref[m].T, 128, 2)
        square[0:64, 0:64] = cc_ref[m]
        send(8 + 2 * m, square[...].T, 64, 2)
    send(16, df.T, 128, 1)
    square[0:64, :] = dc
    send(17, square[...].T, 64, 1)


def rows_kernel(cf_ref, cc_ref, df_ref, dc_ref, fl_ref, fr_ref, up_ref, down_ref, cs_ref, cm_ref, ds_ref, dm_ref, square):
    up_ref[...] = jnp.zeros_like(up_ref)
    down_ref[...] = jnp.zeros_like(down_ref)

    def sides(row, first, width):
        square[...] = jnp.zeros_like(square)
        square[first:first + width, :] = fr_ref[row:row + width, :]
        square[128 - width:128, :] = fl_ref[row:row + width, :]
        return square[...].T

    def send(row, lane, field, size, width):
        lanes = pl.ds(lane, 128)
        up_ref[pl.ds(row, width), lanes] = field[0:width]
        down_ref[pl.ds(row, width), lanes] = field[size - width:size]

    for m in range(4):
        side = sides(2 * m, 0, 2)
        cs_ref[m] = side
        send(2 * m, 0, cf_ref[m], 128, 2)
        send(2 * m, 128, side, 128, 2)
        cm_ref[m] = sides(8 + 2 * m, 64, 2)[0:64]
        cm_ref[m, :, 0:64] = cc_ref[m]
        send(8 + 2 * m, 0, cm_ref[m], 64, 2)
    side = sides(16, 0, 1)
    ds_ref[...] = side
    send(16, 0, df_ref[...], 128, 1)
    send(16, 128, side, 128, 1)
    dm_ref[...] = dc_ref[...] + sides(17, 64, 1)[0:64]
    send(17, 0, dm_ref[...], 64, 1)


def stencil_kernel(cf_ref, cs_ref, cm_ref, df_ref, ds_ref, dm_ref, fu_ref, fd_ref, bf_ref, bc_ref, vf, wf, vc, wc):
    def apply(field, diag):
        rows, lanes = field.shape
        near = pltpu.roll(field, 1, 0) + pltpu.roll(field, rows - 1, 0)
        near = near + (pltpu.roll(field, 1, 1) + pltpu.roll(field, lanes - 1, 1))
        return diag * field - near

    def twice(field, diag):
        first = jnp.where(diag > 0.0, apply(field, diag), 0.0)
        return apply(first, diag)

    def edges(scratch, size, row, width, lanes):
        last = scratch.shape[0]
        scratch[size:last, :] = jnp.zeros((last - size, lanes), F)
        scratch[size:size + width, :] = fd_ref[row:row + width, 0:lanes]
        scratch[last - width:last, :] = fu_ref[row:row + width, 0:lanes]

    wf[0:128, 0:128] = df_ref[...]
    wf[0:128, 128:256] = ds_ref[...]
    edges(wf, 128, 16, 1, 256)
    wc[0:64, :] = dm_ref[...]
    edges(wc, 64, 17, 1, 128)
    for m in range(4):
        vf[0:128, 0:128] = cf_ref[m]
        vf[0:128, 128:256] = cs_ref[m]
        edges(vf, 128, 2 * m, 2, 256)
        bf_ref[m] = twice(vf[...], wf[...])[0:128, 0:128]
        vc[0:64, :] = cm_ref[m]
        edges(vc, 64, 8 + 2 * m, 2, 128)
        bc_ref[m] = twice(vc[...], wc[...])[0:64, 0:64]


def neighbours(axis):
    count = lax.axis_size(axis)
    up = [(i, i + 1) for i in range(count - 1)]
    return up, [(j, i) for i, j in up]


def precision(coef_fine, coef_coarse, kappa_map, kappa_table):
    smem = pl.BlockSpec(memory_space=pltpu.SMEM)
    vmem = pl.BlockSpec(memory_space=pltpu.VMEM)
    square = pltpu.VMEM((128, 128), F)
    to_left, to_right, df, dc = pl.pallas_call(
        columns_kernel,
        in_specs=[smem] + [vmem] * 3,
        out_shape=[struct(24, 128), struct(24, 128), struct(128, 128), struct(64, 128)],
        scratch_shapes=[square],
        compiler_params=params(),
        name="edge_columns",
    )(kappa_table, coef_fine, coef_coarse, kappa_map)
    onward, back = neighbours("tx")
    from_left = lax.ppermute(to_right, "tx", onward)
    from_right = lax.ppermute(to_left, "tx", back)
    to_up, to_down, side, coarse, dside, dcoarse = pl.pallas_call(
        rows_kernel,
        out_shape=[struct(24, 256), struct(24, 256), struct(4, 128, 128), struct(4, 64, 128), struct(128, 128), struct(64, 128)],
        scratch_shapes=[square],
        compiler_params=params(),
        name="edge_rows",
    )(coef_fine, coef_coarse, df, dc, from_left, from_right)
    onward, back = neighbours("ty")
    from_up = lax.ppermute(to_down, "ty", onward)
    from_down = lax.ppermute(to_up, "ty", back)
    return pl.pallas_call(
        stencil_kernel,
        out_shape=[struct(4, 128, 128), struct(4, 64, 64)],
        scratch_shapes=[pltpu.VMEM((136, 256), F), pltpu.VMEM((136, 256), F), pltpu.VMEM((72, 128), F), pltpu.VMEM((72, 128), F)],
        compiler_params=params(),
        name="stencil_twice",
    )(coef_fine, side, coarse, df, dside, dcoarse, from_up, from_down)


def spline(t):
    s = 1.0 - t
    return (
        s * s * s / 6.0,
        (3.0 * t * t * t - 6.0 * t * t + 4.0) / 6.0,
        (-3.0 * t * t * t + 3.0 * t * t + 3.0 * t + 1.0) / 6.0,
        t * t * t / 6.0,
    )


def rotate(weights, start):
    odd = (start & 1) == 1
    weights = [jnp.where(odd, weights[(r - 1) % 4], weights[r]) for r in range(4)]
    two = (start & 2) == 2
    return [jnp.where(two, weights[(r - 2) % 4], weights[r]) for r in range(4)]


def project_kernel(steps, group, slots, lw_ref, v_ref, off_ref, pos_ref, bf_ref, bc_ref, fine_ref, coarse_ref, rows, acc):
    step = pl.program_id(0)

    @pl.when(step == 0)
    def _():
        acc[...] = jnp.zeros_like(acc)

    chunks = slots // 128
    sy = off_ref[0] - 2
    sx = off_ref[1] - 2
    upper = sy >= 61
    sy = jnp.where(upper, sy - 61, sy)
    by = sy & 3
    bx = sx & 3
    qy = sy >> 2
    qx = (sx >> 2) + jnp.where(upper, 32, 0)
    wy = rotate(spline(pos_ref[0]), by)
    wx = rotate(spline(pos_ref[1]), bx)
    for r in range(4):
        rows[r] = (qy + jnp.where(by > r, 1, 0)).astype(F)
        rows[4 + r] = (qx + jnp.where(bx > r, 1, 0)).astype(F)
        rows[8 + r] = wx[r]
    for m in range(4):
        v = jnp.concatenate([v_ref[pl.ds(4 * kc + m, group, stride=4 * chunks), :] for kc in range(chunks)], 1)
        for r in range(4):
            rows[12 + 4 * m + r] = v * wy[r]
    i16 = iota((16, slots), 0).astype(F).astype(BF)
    i64 = iota((64, slots), 0).astype(F).astype(BF)
    zero = jnp.zeros((), BF)

    def spread(i, s, n):
        row = jnp.broadcast_to(rows[i, pl.ds(s, 1), :], (16, slots)).astype(BF)
        return jnp.broadcast_to(row[None], (n // 16, 16, slots)).reshape(n, slots)

    for s in range(group):
        left = [None] * 16
        for r in range(4):
            here = i16 == spread(r, s, 16)
            for m in range(4):
                left[4 * m + r] = jnp.where(here, spread(12 + 4 * m + r, s, 16), zero)
        right = [jnp.where(i64 == spread(4 + r, s, 64), spread(8 + r, s, 64), zero) for r in range(4)]
        acc[...] += mm(jnp.concatenate(left, 0), jnp.concatenate(right, 0), ((1,), (1,)))

    @pl.when(step == steps - 1)
    def _():
        a = iota((256, 256), 0)
        b = iota((256, 256), 1)
        place = ((b >> 7) == ((a >> 5) & 1)) & ((b & 127) == 1 + 4 * (a & 31) + (a >> 6))
        place = jnp.where(place, 1.0, 0.0).astype(BF)
        wide = sum(mm(p, place) for p in split3(acc[...]))
        ya = iota((128, 64), 0)
        yb = iota((128, 64), 1)
        row = 1 + 4 * (yb & 15) + (yb >> 4)
        lift = [jnp.where(ya == row + 61 * h, 1.0, 0.0).astype(BF) for h in range(2)]
        far = jnp.abs(iota((64, 128), 1) - 2 * iota((64, 128), 0))
        halve = jnp.where(far == 0, 0.75, jnp.where(far == 1, 0.5, jnp.where(far == 2, 0.125, 0.0))).astype(BF)
        for m in range(4):
            part = wide[m * 64:(m + 1) * 64]
            fine = sum(mm(lift[h], p) for h in range(2) for p in split3(part[:, h * 128:(h + 1) * 128]))
            fine_ref[m] = lw_ref[0] * fine - bf_ref[m]
            coarse = sum(mm(halve, p) for p in split3(fine))
            coarse = sum(mm(p, halve, ((1,), (1,))) for p in split3(coarse))
            coarse_ref[m] = lw_ref[1] * coarse - bc_ref[m]


def project(values, offsets, positions, level_weight, fine, coarse):
    tiles, slots = offsets.shape[1:]
    group = 16
    steps = tiles // group
    whole = [pl.BlockSpec((4, 128, 128), lambda i: (0, 0, 0)), pl.BlockSpec((4, 64, 64), lambda i: (0, 0, 0))]
    return pl.pallas_call(
        functools.partial(project_kernel, steps, group, slots),
        grid=(steps,),
        in_specs=[
            pl.BlockSpec(memory_space=pltpu.SMEM),
            pl.BlockSpec((group * slots // 32, 128), lambda i: (i, 0)),
            pl.BlockSpec((2, group, slots), lambda i: (0, i, 0)),
            pl.BlockSpec((2, group, slots), lambda i: (0, i, 0)),
        ] + whole,
        out_specs=whole,
        out_shape=[struct(4, 128, 128), struct(4, 64, 64)],
        scratch_shapes=[pltpu.VMEM((28, group, slots), F), pltpu.VMEM((256, 256), F)],
        compiler_params=params(),
        name="project_rows",
    )(level_weight, values, offsets, positions, fine, coarse)


def on_device(residual, counts, offsets, positions, coef_fine, coef_coarse, kappa_map, kappa_table, level_weight):
    tiles = residual.shape[2]
    packed = pack(counts, residual[0])
    packed = packed.reshape(tiles, -1, 128)
    arrived = lax.all_to_all(packed, AXES, split_axis=0, concat_axis=0, tiled=True)
    fine, coarse = precision(coef_fine, coef_coarse, kappa_map, kappa_table)
    return tuple(project(arrived.reshape(-1, 128), offsets[0], positions[0], level_weight, fine, coarse))


def solution(mesh):
    rows = P(AXES, None, None, None)
    tile = P(None, "ty", "tx")
    return jax.shard_map(
        on_device,
        mesh=mesh,
        in_specs=(rows, P(AXES, None), rows, rows, tile, tile, P("ty", "tx"), P(), P()),
        out_specs=(tile, tile),
        check_vma=False,
    )
```

time: 472 us -> 68.7 us (0.15); the launches traced: 466 us -> 68.3 us
  other arithmetic: 146 us -> 0 us
  local copies, waits for them, and re-layouts: 150 us -> 4.55 us
  matrix products: 90.1 us -> 0 us
  starting transfers between devices: 60.6 us -> 23.6 us
  Pallas kernels: 0 us -> 24.6 us
    while x32 -> x0, local copies, waits for them, and re-layouts: 129 us -> none
    convert_element_type x32 -> x0, other arithmetic: 93.1 us -> none  [the longest x16 55.3 us: add_block(): right = column_x.astype(jnp.bfloat16).reshape(side, group * slots)]
    dot_general x16 -> x0, matrix products: 90.1 us -> none  [add_block(): lax.dot_general(left, right, (((1,), (1,)), ((), ())), preferred_element_...]
    ppermute x16 -> x4, starting transfers between devices: 50.1 us -> 13.1 us  [the longest x1 5.12 us: precision(): from_up = lax.ppermute(to_down, 'ty', onward)]
    pallas_call x0 -> x5, Pallas kernels: none -> 24.6 us  [the longest x1 20.2 us: project(): pl.pallas_call(functools.partial(project_kernel, steps, group, slots), gr...]
    dynamic_slice x16 -> x0, local copies, waits for them, and re-layouts: 15.2 us -> none  [add_block(): block_values = lax.dynamic_slice_in_dim(values, first, group, 1)]
    broadcast_in_dim x16 -> x0, other arithmetic: 14.5 us -> none  [add_block(): jnp.where(lattice == block_cells[1][None] - 1 + a, weight_x[a][None], 0.0)]
    eq x16 -> x0, other arithmetic: 13.7 us -> none  [add_block(): lattice == block_cells[1][None] - 1 + a]
  transfers between devices with their start and end apart: 17 -> 5, of which waited for: 4 -> 3; matrix products, arithmetic and copies ran while one was open for 82% -> 0% of each run, Pallas kernels for 0% -> 3%
where the time goes in v1:
time: 68.7 us; the launch traced here: 68.3 us
  Pallas kernels  24.6 us (36%)
  starting transfers between devices  23.6 us (34%)
  waiting for transfers between devices  14.8 us (22%)
  local copies, waits for them, and re-layouts  4.55 us (7%)
  between operations  0.77 us (1%)
    pallas_call x1, Pallas kernels, project(): pl.pallas_call(functools.partial(project_kernel, steps, group, slots), gr...  20.2 us
    all_to_all x1, starting transfers between devices, on_device(): lax.all_to_all(packed, AXES, split_axis=0, concat_axis=0, tiled=True)  10.5 us
    ppermute x1, waiting for transfers between devices, precision(): from_left = lax.ppermute(to_right, 'tx', onward)  9.99 us
    ppermute x1, starting transfers between devices, precision(): from_up = lax.ppermute(to_down, 'ty', onward)  5.12 us
    unnamed x22, local copies, waits for them, and re-layouts  4.55 us
    ppermute x1, starting transfers between devices, precision(): from_left = lax.ppermute(to_right, 'tx', onward)  4.18 us
    ppermute x1, waiting for transfers between devices, precision(): from_down = lax.ppermute(to_up, 'ty', back)  4.11 us
    pallas_call x1, Pallas kernels, pack(): pl.pallas_call(functools.partial(pack_kernel, block), grid=(tiles // bloc...  2.04 us
  transfers between devices with their start and end apart: 5, of which 3 were waited for; matrix products, arithmetic and copies ran while one was open for 0% of the time, Pallas kernels for 3%

profile of v1, /device:TPU:39, one launch (start us, length us, event | category | flops | bytes accessed | tf_op | source)
XLA Modules:
  0.0 68.3 jit_solution(7686120480453120153)
XLA Ops:
  0.6 0.0 copy-start.1
  0.6 1.4 %copy-done.1 = f32[1,4,128,768]{3,2,1,0:T(8,128)S(1)} copy-done((f32[1,4,128,768]{3,2,1,0:T(8,128)S(1)}, f32[1,4,128,768]{3,2,1,0:T(8,128)}, u32[]{:S(2)}) %copy-start.1) | copy-done | bytes 1572888
  2.0 0.0 copy-start.9
  2.0 0.7 copy-done.9
  2.7 2.0 %pack_rows.1 = f32[3072,128]{1,0:T(8,128)} custom-call(s32[1,128]{1,0:T(1,128)S(1)} %copy-done.9, f32[4,128,768]{2,1,0:T(8,128)S(1)} %bitcast.6), custom_call_target="tpu_custom_call" | custom-call | tf_op jit(solution)/shard_map/pack_rows/pallas_call | solution.py:59
  4.7 0.0 copy-start
  4.7 10.5 %all-to-all-start = ((f32[128,24,128]{2,1,0:T(8,128)}), f32[128,24,128]{2,1,0:T(8,128)S(1)}, u32[]{:S(2)}, u32[]{:S(2)}) async-start(f32[128,24,128]{2,1,0:T(8,128)} %bitcast.1), calls=%async_computation | async-start | bytes 3145728 | tf_op jit(solution)/shard_map/all_to_all | solution.py:316
  15.2 0.0 copy-done
  15.3 0.0 copy-done.4
  15.3 0.0 copy-done.8
  15.3 0.0 copy-start.7
  15.3 0.8 %copy-done.7 = s32[128,128]{1,0:T(8,128)S(1)} copy-done((s32[128,128]{1,0:T(8,128)S(1)}, s32[128,128]{1,0:T(8,128)}, u32[]{:S(2)}) %copy-start.7) | copy-done | bytes 65560
  16.1 0.8 %edge_columns.1 = (f32[24,128]{1,0:T(8,128)S(1)}, f32[24,128]{1,0:T(8,128)S(1)}, f32[128,128]{1,0:T(8,128)S(1)}, f32[64,128]{1,0:T(8,128)S(1)}) custom-call(f32[2,8]{1,0:T(2,128)S(1)} %copy-done.8, f32[4,128,128]{2,1,0:T(8,128)S(1)} %copy-done, f32[4,64,64]{2,1,0:T(8,128)S(1)} %copy-done.4, s32[128,128]{1,0:T(8,128)S(1)} %copy-done.7), custom_call_target="tpu_custom_call" | custom-call | tf_op jit(solution)/shard_map/edge_columns/pallas_call | solution.py:178
  16.9 4.2 %collective-permute-start = (f32[24,128]{1,0:T(8,128)S(1)}, f32[24,128]{1,0:T(8,128)S(1)}, u32[]{:S(2)}, u32[]{:S(2)}) collective-permute-start(f32[24,128]{1,0:T(8,128)S(1)} %get-tuple-element.16), channel_id=1, source_target_pairs={{0,1},{1,2},{2,3},{3,4},{4,5},{5,6},{6,7},{8,9},{9,10},{10,11},{11... | collective-permute-start | bytes 36872 | tf_op jit(solution)/shard_map/ppermute | solution.py:187
  21.1 1.9 %collective-permute-start.1 = (f32[24,128]{1,0:T(8,128)S(1)}, f32[24,128]{1,0:T(8,128)S(1)}, u32[]{:S(2)}, u32[]{:S(2)}) collective-permute-start(f32[24,128]{1,0:T(8,128)S(1)} %get-tuple-element.17), channel_id=1, source_target_pairs={{1,0},{2,1},{3,2},{4,3},{5,4},{6,5},{7,6},{9,8},{10,9},{11,10},{12... | collective-permute-start | bytes 36872 | tf_op jit(solution)/shard_map/ppermute | solution.py:188
  23.0 10.0 %collective-permute-done.fl_ref = f32[24,128]{1,0:T(8,128)S(1)} collective-permute-done((f32[24,128]{1,0:T(8,128)S(1)}, f32[24,128]{1,0:T(8,128)S(1)}, u32[]{:S(2)}, u32[]{:S(2)}) %collective-permute-start) | collective-permute-done | bytes 12320 | tf_op jit(solution)/shard_map/ppermute | solution.py:187
  33.0 0.7 collective-permute-done.1.fr_ref
  33.7 0.3 edge_rows.1
  34.0 5.1 %collective-permute-start.2 = (f32[24,256]{1,0:T(8,128)S(1)}, f32[24,256]{1,0:T(8,128)S(1)}, u32[]{:S(2)}, u32[]{:S(2)}) collective-permute-start(f32[24,256]{1,0:T(8,128)S(1)} %get-tuple-element.22), channel_id=1, source_target_pairs={{0,8},{8,16},{16,24},{24,32},{32,40},{40,48},{48,56},{56,64},{64,7... | collective-permute-start | bytes 73736 | tf_op jit(solution)/shard_map/ppermute | solution.py:197
  39.1 1.9 %collective-permute-start.3 = (f32[24,256]{1,0:T(8,128)S(1)}, f32[24,256]{1,0:T(8,128)S(1)}, u32[]{:S(2)}, u32[]{:S(2)}) collective-permute-start(f32[24,256]{1,0:T(8,128)S(1)} %get-tuple-element.23), channel_id=1, source_target_pairs={{8,0},{16,8},{24,16},{32,24},{40,32},{48,40},{56,48},{64,56},{72,6... | collective-permute-start | bytes 73736 | tf_op jit(solution)/shard_map/ppermute | solution.py:198
  41.0 0.0 collective-permute-done.2.fu_ref
  41.0 4.1 %collective-permute-done.3.fd_ref = f32[24,256]{1,0:T(8,128)S(1)} collective-permute-done((f32[24,256]{1,0:T(8,128)S(1)}, f32[24,256]{1,0:T(8,128)S(1)}, u32[]{:S(2)}, u32[]{:S(2)}) %collective-permute-start.3) | collective-permute-done | bytes 24608 | tf_op jit(solution)/shard_map/ppermute | solution.py:198
  45.1 1.2 %stencil_twice.1 = (f32[4,128,128]{2,1,0:T(8,128)S(1)}, f32[4,64,64]{2,1,0:T(8,128)S(1)}) custom-call(f32[4,128,128]{2,1,0:T(8,128)S(1)} %copy-done, f32[4,128,128]{2,1,0:T(8,128)S(1)} %get-tuple-element.18.cs_ref, f32[4,64,128]{2,1,0:T(8,128)S(1)} %get-tuple-element.19.cm_ref, f32[128,128]{1,0:T(8,128)S(1)} %get-tuple-element.14.df_ref, ...), custom_call_target="tpu_custom_call" | custom-call | tf_op jit(solution)/shard_map/stencil_twice/pallas_call | solution.py:199
  46.4 0.0 copy-start.5
  46.4 0.7 %copy-done.5 = f32[4,128,128]{2,1,0:T(8,128)} copy-done((f32[4,128,128]{2,1,0:T(8,128)}, f32[4,128,128]{2,1,0:T(8,128)S(1)}, u32[]{:S(2)}) %copy-start.5) | copy-done | bytes 262168
  47.1 0.0 all-to-all-done
  47.1 0.0 copy-done.2
  47.1 0.0 copy-done.3
  47.1 0.0 copy-done.10
  47.1 0.0 copy-start.6
  47.1 0.9 %copy-done.6 = f32[4,128,128]{2,1,0:T(8,128)S(1)} copy-done((f32[4,128,128]{2,1,0:T(8,128)S(1)}, f32[4,128,128]{2,1,0:T(8,128)}, u32[]{:S(2)}) %copy-start.6) | copy-done | bytes 262168
  48.1 20.2 %project_rows.1 = (f32[4,128,128]{2,1,0:T(8,128)}, f32[4,64,64]{2,1,0:T(8,128)}) custom-call(f32[2]{0:T(128)S(1)} %copy-done.10, f32[3072,128]{1,0:T(8,128)S(1)} %bitcast.5, s32[2,128,768]{2,1,0:T(8,128)S(1)} %bitcast.7, f32[2,128,768]{2,1,0:T(8,128)S(1)} %bitcast.8, f32[4,128,128]{2,1,0:T(8,128)S(1)} %copy-done.6, f32[4,64,64]{2,1,0:T(8,128)S(1)} %get-tuple-element.25.bc_ref), custom_call_target="tpu_custom_call" | custom-call | tf_op jit(solution)/shard_map/project_rows/pallas_call | solution.py:295
  (5 shorter events, 0.0 us)
Async XLA Ops:
  0.6 1.4 %copy-start.1 = (f32[1,4,128,768]{3,2,1,0:T(8,128)S(1)}, f32[1,4,128,768]{3,2,1,0:T(8,128)}, u32[]{:S(2)}) copy-start(f32[1,4,128,768]{3,2,1,0:T(8,128)} %param.9) | copy-start | bytes 4718596
  2.0 0.7 copy-start.9
  4.7 10.5 %copy-start = (f32[4,128,128]{2,1,0:T(8,128)S(1)}, f32[4,128,128]{2,1,0:T(8,128)}, u32[]{:S(2)}) copy-start(f32[4,128,128]{2,1,0:T(8,128)} %cf_ref.5) | copy-start | bytes 786436
  4.7 10.5 %copy-start.4 = (f32[4,64,64]{2,1,0:T(8,128)S(1)}, f32[4,64,64]{2,1,0:T(8,128)}, u32[]{:S(2)}) copy-start(f32[4,64,64]{2,1,0:T(8,128)} %cc_ref.3) | copy-start | bytes 196612
  4.7 10.5 %copy-start.8 = (f32[2,8]{1,0:T(2,128)S(1)}, f32[2,8]{1,0:T(2,128)}, u32[]{:S(2)}) copy-start(f32[2,8]{1,0:T(2,128)} %table_ref.1) | copy-start | bytes 196
  4.7 42.4 %all-to-all-start = ((f32[128,24,128]{2,1,0:T(8,128)}), f32[128,24,128]{2,1,0:T(8,128)S(1)}, u32[]{:S(2)}, u32[]{:S(2)}) async-start(f32[128,24,128]{2,1,0:T(8,128)} %bitcast.1), calls=%async_computation | async-start | bytes 3145728 | tf_op jit(solution)/shard_map/all_to_all | solution.py:316
  15.3 0.8 %copy-start.7 = (s32[128,128]{1,0:T(8,128)S(1)}, s32[128,128]{1,0:T(8,128)}, u32[]{:S(2)}) copy-start(s32[128,128]{1,0:T(8,128)} %km_ref.1) | copy-start | bytes 196612
  16.1 31.0 %copy-start.2 = (s32[1,2,128,768]{3,2,1,0:T(8,128)S(1)}, s32[1,2,128,768]{3,2,1,0:T(8,128)}, u32[]{:S(2)}) copy-start(s32[1,2,128,768]{3,2,1,0:T(8,128)} %param.11) | copy-start | bytes 2359300
  16.1 31.0 %copy-start.3 = (f32[1,2,128,768]{3,2,1,0:T(8,128)S(1)}, f32[1,2,128,768]{3,2,1,0:T(8,128)}, u32[]{:S(2)}) copy-start(f32[1,2,128,768]{3,2,1,0:T(8,128)} %param.12) | copy-start | bytes 2359300
  16.1 31.0 %copy-start.10 = (f32[2]{0:T(128)S(1)}, f32[2]{0:T(128)}, u32[]{:S(2)}) copy-start(f32[2]{0:T(128)} %lw_ref.1) | copy-start | bytes 28
  16.9 16.1 %collective-permute-start = (f32[24,128]{1,0:T(8,128)S(1)}, f32[24,128]{1,0:T(8,128)S(1)}, u32[]{:S(2)}, u32[]{:S(2)}) collective-permute-start(f32[24,128]{1,0:T(8,128)S(1)} %get-tuple-element.16), channel_id=1, source_target_pairs={{0,1},{1,2},{2,3},{3,4},{4,5},{5,6},{6,7},{8,9},{9,10},{10,11},{11... | collective-permute-start | bytes 36872 | tf_op jit(solution)/shard_map/ppermute | solution.py:187
  21.1 12.6 %collective-permute-start.1 = (f32[24,128]{1,0:T(8,128)S(1)}, f32[24,128]{1,0:T(8,128)S(1)}, u32[]{:S(2)}, u32[]{:S(2)}) collective-permute-start(f32[24,128]{1,0:T(8,128)S(1)} %get-tuple-element.17), channel_id=1, source_target_pairs={{1,0},{2,1},{3,2},{4,3},{5,4},{6,5},{7,6},{9,8},{10,9},{11,10},{12... | collective-permute-start | bytes 36872 | tf_op jit(solution)/shard_map/ppermute | solution.py:188
  34.0 7.1 %collective-permute-start.2 = (f32[24,256]{1,0:T(8,128)S(1)}, f32[24,256]{1,0:T(8,128)S(1)}, u32[]{:S(2)}, u32[]{:S(2)}) collective-permute-start(f32[24,256]{1,0:T(8,128)S(1)} %get-tuple-element.22), channel_id=1, source_target_pairs={{0,8},{8,16},{16,24},{24,32},{32,40},{40,48},{48,56},{56,64},{64,7... | collective-permute-start | bytes 73736 | tf_op jit(solution)/shard_map/ppermute | solution.py:197
  39.1 6.0 %collective-permute-start.3 = (f32[24,256]{1,0:T(8,128)S(1)}, f32[24,256]{1,0:T(8,128)S(1)}, u32[]{:S(2)}, u32[]{:S(2)}) collective-permute-start(f32[24,256]{1,0:T(8,128)S(1)} %get-tuple-element.23), channel_id=1, source_target_pairs={{8,0},{16,8},{24,16},{32,24},{40,32},{48,40},{56,48},{64,56},{72,6... | collective-permute-start | bytes 73736 | tf_op jit(solution)/shard_map/ppermute | solution.py:198
  46.4 0.7 %copy-start.5 = (f32[4,128,128]{2,1,0:T(8,128)}, f32[4,128,128]{2,1,0:T(8,128)S(1)}, u32[]{:S(2)}) copy-start(f32[4,128,128]{2,1,0:T(8,128)S(1)} %get-tuple-element.24.bf_ref) | copy-start | bytes 786436
  47.1 1.0 %copy-start.6 = (f32[4,128,128]{2,1,0:T(8,128)S(1)}, f32[4,128,128]{2,1,0:T(8,128)}, u32[]{:S(2)}) copy-start(f32[4,128,128]{2,1,0:T(8,128)} %copy-done.5) | copy-start | bytes 786436

commit v2 on v1

v2 whole, which is shorter than its diff:
```python
import functools

import jax
import jax.numpy as jnp
from jax import lax
from jax.experimental import pallas as pl
from jax.experimental.pallas import tpu as pltpu
from jax.sharding import PartitionSpec as P

BF = jnp.bfloat16
F = jnp.float32
VMEM_LIMIT = 48 * 1024 * 1024
AXES = ("ty", "tx")


def struct(*shape):
    return jax.ShapeDtypeStruct(shape, F)


def iota(shape, dim):
    return lax.broadcasted_iota(jnp.int32, shape, dim)


def mm(a, b, dims=((1,), (0,))):
    return lax.dot_general(a, b, (dims, ((), ())), preferred_element_type=F)


def split3(a):
    hi = a.astype(BF)
    a = a - hi.astype(F)
    mid = a.astype(BF)
    lo = (a - mid.astype(F)).astype(BF)
    return hi, mid, lo


def params():
    return pltpu.CompilerParams(vmem_limit_bytes=VMEM_LIMIT)


def pack_kernel(block, counts_ref, res_ref, out_ref, loaded, built, sems, out_sems):
    tiles, slots = res_ref.shape[1:]
    parts = tiles // block
    chunks = slots // 128
    rows = 4 * chunks * block
    loads = [
        pltpu.make_async_copy(res_ref.at[:, pl.ds(i * block, block), :], loaded.at[i], sems.at[i]) for i in range(parts)
    ]
    for load in loads:
        load.start()
    stores = []
    for i in range(parts):
        loads[i].wait()
        for d in range(0, block, 8):
            live = jnp.zeros((8, 128), jnp.int32)
            for j in range(8):
                live = jnp.where(iota((8, 128), 0) == j, counts_ref[0, i * block + d + j], live)
            for kc in range(chunks):
                keep = iota((8, 128), 1) + 128 * kc < live
                for m in range(4):
                    row = (d * chunks + kc) * 4 + m
                    value = jnp.where(keep, loaded[i, m, d:d + 8, 128 * kc:128 * kc + 128], 0.0)
                    built[i, pl.ds(row, 8, stride=4 * chunks), :] = value
        store = pltpu.make_async_copy(built.at[i], out_ref.at[pl.ds(i * rows, rows), :], out_sems.at[i])
        store.start()
        stores.append(store)
    for store in stores:
        store.wait()


def pack(counts, residual):
    channels, tiles, slots = residual.shape
    block = 16
    parts = tiles // block
    rows = 4 * (slots // 128)
    return pl.pallas_call(
        functools.partial(pack_kernel, block),
        in_specs=[pl.BlockSpec(memory_space=pltpu.SMEM), pl.BlockSpec(memory_space=pltpu.HBM)],
        out_specs=pl.BlockSpec(memory_space=pl.ANY),
        out_shape=struct(tiles * rows, 128),
        scratch_shapes=[
            pltpu.VMEM((parts, channels, block, slots), F),
            pltpu.VMEM((parts, block * rows, 128), F),
            pltpu.SemaphoreType.DMA((parts,)),
            pltpu.SemaphoreType.DMA((parts,)),
        ],
        compiler_params=pltpu.CompilerParams(vmem_limit_bytes=62 * 1024 * 1024),
        name="pack_rows",
    )(counts, residual)


def classes_to_diag(kinds, table_ref, level):
    total = jnp.zeros(kinds.shape, F)
    for k in range(table_ref.shape[1]):
        total = jnp.where(kinds == k, table_ref[level, k], total)
    return 4.0 + total


def columns_kernel(table_ref, cf_ref, cc_ref, km_ref, left_ref, right_ref, df_ref, dc_ref, square):
    left_ref[...] = jnp.zeros_like(left_ref)
    right_ref[...] = jnp.zeros_like(right_ref)
    square[...] = jnp.zeros_like(square)
    df = classes_to_diag(km_ref[...], table_ref, 0)
    df_ref[...] = df
    even = km_ref[pl.ds(0, 64, stride=2), :].astype(F).astype(BF)
    pick = jnp.where(iota((128, 128), 0) == 2 * iota((128, 128), 1), 1.0, 0.0).astype(BF)
    dc = classes_to_diag(mm(even, pick).astype(jnp.int32), table_ref, 1)
    dc = jnp.where(iota((64, 128), 1) < 64, dc, 0.0)
    dc_ref[...] = dc

    def send(row, turned, size, width):
        left_ref[pl.ds(row, width), :] = turned[0:width]
        right_ref[pl.ds(row, width), :] = turned[size - width:size]

    for m in range(4):
        send(2 * m, cf_ref[m].T, 128, 2)
        square[0:64, 0:64] = cc_ref[m]
        send(8 + 2 * m, square[...].T, 64, 2)
    send(16, df.T, 128, 1)
    square[0:64, :] = dc
    send(17, square[...].T, 64, 1)


def rows_kernel(cf_ref, cc_ref, df_ref, dc_ref, fl_ref, fr_ref, at_ref, up_ref, down_ref, cs_ref, cm_ref, ds_ref, dm_ref, square):
    up_ref[...] = jnp.zeros_like(up_ref)
    down_ref[...] = jnp.zeros_like(down_ref)

    def sides(row, first, width):
        square[...] = jnp.zeros_like(square)
        square[first:first + width, :] = fr_ref[row:row + width, :]
        square[128 - width:128, :] = fl_ref[row:row + width, :]
        return square[...].T

    def send(row, lane, field, size, width):
        lanes = pl.ds(lane, 128)
        up_ref[pl.ds(row, width), lanes] = field[0:width]
        down_ref[pl.ds(row, width), lanes] = field[size - width:size]

    for m in range(4):
        side = sides(2 * m, 0, 2)
        cs_ref[m] = side
        send(2 * m, 0, cf_ref[m], 128, 2)
        send(2 * m, 128, side, 128, 2)
        cm_ref[m] = sides(8 + 2 * m, 64, 2)[0:64]
        cm_ref[m, :, 0:64] = cc_ref[m]
        send(8 + 2 * m, 0, cm_ref[m], 64, 2)
    side = sides(16, 0, 1)
    ds_ref[...] = side
    send(16, 0, df_ref[...], 128, 1)
    send(16, 128, side, 128, 1)
    dm_ref[...] = dc_ref[...] + sides(17, 64, 1)[0:64]
    send(17, 0, dm_ref[...], 64, 1)


def finish_kernel(lw_ref, acc, cf_ref, cs_ref, cm_ref, df_ref, ds_ref, dm_ref, fu_ref, fd_ref, fine_ref, coarse_ref, vf, wf, vc, wc, tall, low):
    def apply(field, diag):
        rows, lanes = field.shape
        near = pltpu.roll(field, 1, 0) + pltpu.roll(field, rows - 1, 0)
        near = near + (pltpu.roll(field, 1, 1) + pltpu.roll(field, lanes - 1, 1))
        return diag * field - near

    def twice(field, diag):
        first = jnp.where(diag > 0.0, apply(field, diag), 0.0)
        return apply(first, diag)

    def rim(scratch, size, row, width, lanes):
        last = scratch.shape[0]
        scratch[size:last, :] = jnp.zeros((last - size, lanes), F)
        scratch[size:size + width, :] = fd_ref[row:row + width, 0:lanes]
        scratch[last - width:last, :] = fu_ref[row:row + width, 0:lanes]

    wf[0:128, 0:128] = df_ref[...]
    wf[0:128, 128:256] = ds_ref[...]
    rim(wf, 128, 16, 1, 256)
    wc[0:64, :] = dm_ref[...]
    rim(wc, 64, 17, 1, 128)
    for m in range(4):
        vf[0:128, 0:128] = cf_ref[m]
        vf[0:128, 128:256] = cs_ref[m]
        rim(vf, 128, 2 * m, 2, 256)
        fine_ref[m] = twice(vf[...], wf[...])[0:128, 0:128]
        vc[0:64, :] = cm_ref[m]
        rim(vc, 64, 8 + 2 * m, 2, 128)
        coarse_ref[m] = twice(vc[...], wc[...])[0:64, 0:64]

    a = iota((256, 256), 0)
    b = iota((256, 256), 1)
    place = ((b >> 7) == ((a >> 5) & 1)) & ((b & 127) == 1 + 4 * (a & 31) + (a >> 6))
    place = jnp.where(place, 1.0, 0.0).astype(BF)
    wide = sum(mm(p, place) for p in split3(acc[...]))
    far = jnp.abs(iota((128, 128), 0) - 2 * iota((128, 128), 1))
    halve = jnp.where(far == 0, 0.75, jnp.where(far == 1, 0.5, jnp.where(far == 2, 0.125, 0.0))).astype(BF)
    for m in range(4):
        tall[m, 0:16, :] = jnp.zeros((16, 128), F)
        tall[m, 72:144, :] = jnp.zeros((72, 128), F)
        for h in range(2):
            for r in range(4):
                at = m * 64 + r * 16
                spots = pl.ds(9 + 61 * h + r, 16, stride=4)
                part = wide[at:at + 16, h * 128:(h + 1) * 128]
                tall[m, spots, :] = part if h == 0 else part + tall[m, spots, :]
        fine_ref[m] = lw_ref[0] * tall[m, 8:136, :] - fine_ref[m]
        every = [tall[m, pl.ds(8 + k, 64, stride=2), :] for k in range(-2, 3)]
        low[m * 64:(m + 1) * 64, :] = 0.75 * every[2] + 0.5 * (every[1] + every[3]) + 0.125 * (every[0] + every[4])
    coarse = sum(mm(p, halve) for p in split3(low[...]))
    for m in range(4):
        coarse_ref[m] = lw_ref[1] * coarse[m * 64:(m + 1) * 64, 0:64] - coarse_ref[m]


def neighbours(axis):
    count = lax.axis_size(axis)
    up = [(i, i + 1) for i in range(count - 1)]
    return up, [(j, i) for i, j in up]


def edges(coef_fine, coef_coarse, kappa_map, kappa_table, at):
    smem = pl.BlockSpec(memory_space=pltpu.SMEM)
    vmem = pl.BlockSpec(memory_space=pltpu.VMEM)
    square = pltpu.VMEM((128, 128), F)
    to_left, to_right, df, dc = pl.pallas_call(
        columns_kernel,
        in_specs=[smem] + [vmem] * 3,
        out_shape=[struct(24, 128), struct(24, 128), struct(128, 128), struct(64, 128)],
        scratch_shapes=[square],
        compiler_params=params(),
        name="edge_columns",
    )(kappa_table, coef_fine, coef_coarse, kappa_map)
    onward, back = neighbours("tx")
    from_left = lax.ppermute(to_right, "tx", onward)
    from_right = lax.ppermute(to_left, "tx", back)
    to_up, to_down, side, coarse, dside, dcoarse = pl.pallas_call(
        rows_kernel,
        in_specs=[vmem] * 6 + [pl.BlockSpec(memory_space=pl.ANY)],
        out_shape=[struct(24, 256), struct(24, 256), struct(4, 128, 128), struct(4, 64, 128), struct(128, 128), struct(64, 128)],
        scratch_shapes=[square],
        compiler_params=params(),
        name="edge_rows",
    )(coef_fine, coef_coarse, df, dc, from_left, from_right, at)
    onward, back = neighbours("ty")
    from_up = lax.ppermute(to_down, "ty", onward)
    from_down = lax.ppermute(to_up, "ty", back)
    return coef_fine, side, coarse, df, dside, dcoarse, from_up, from_down


def finish(level_weight, total, fields):
    vmem = pl.BlockSpec(memory_space=pltpu.VMEM)
    return pl.pallas_call(
        finish_kernel,
        in_specs=[pl.BlockSpec(memory_space=pltpu.SMEM)] + [vmem] * (1 + len(fields)),
        out_shape=[struct(4, 128, 128), struct(4, 64, 64)],
        scratch_shapes=[
            pltpu.VMEM((136, 256), F),
            pltpu.VMEM((136, 256), F),
            pltpu.VMEM((72, 128), F),
            pltpu.VMEM((72, 128), F),
            pltpu.VMEM((4, 144, 128), F),
            pltpu.VMEM((256, 128), F),
        ],
        compiler_params=params(),
        name="finish_tiles",
    )(level_weight, total, *fields)


def spline(t):
    s = 1.0 - t
    return (
        s * s * s / 6.0,
        (3.0 * t * t * t - 6.0 * t * t + 4.0) / 6.0,
        (-3.0 * t * t * t + 3.0 * t * t + 3.0 * t + 1.0) / 6.0,
        t * t * t / 6.0,
    )


def rotate(weights, start):
    odd = (start & 1) == 1
    weights = [jnp.where(odd, weights[(r - 1) % 4], weights[r]) for r in range(4)]
    two = (start & 2) == 2
    return [jnp.where(two, weights[(r - 2) % 4], weights[r]) for r in range(4)]


def place_kernel(off_ref, pos_ref, out_ref):
    sy = off_ref[0] - 2
    sx = off_ref[1] - 2
    upper = sy >= 61
    sy = jnp.where(upper, sy - 61, sy)
    by = sy & 3
    bx = sx & 3
    qy = sy >> 2
    qx = (sx >> 2) + jnp.where(upper, 32, 0)
    wy = rotate(spline(pos_ref[0]), by)
    wx = rotate(spline(pos_ref[1]), bx)
    for r in range(4):
        out_ref[r] = (qy + jnp.where(by > r, 1, 0)).astype(F)
        out_ref[4 + r] = (qx + jnp.where(bx > r, 1, 0)).astype(F)
        out_ref[8 + r] = wx[r]
        out_ref[12 + r] = wy[r]


def places(offsets, positions):
    tiles, slots = offsets.shape[1:]
    group = 16
    points = pl.BlockSpec((2, group, slots), lambda i: (0, i, 0))
    return pl.pallas_call(
        place_kernel,
        grid=(tiles // group,),
        in_specs=[points, points],
        out_specs=pl.BlockSpec((16, group, slots), lambda i: (0, i, 0)),
        out_shape=struct(16, tiles, slots),
        compiler_params=params(),
        name="place_rows",
    )(offsets, positions)


def project_kernel(group, slots, v_ref, at_ref, acc, values):
    @pl.when(pl.program_id(0) == 0)
    def _():
        acc[...] = jnp.zeros_like(acc)

    chunks = slots // 128
    for m in range(4):
        v = jnp.concatenate([v_ref[pl.ds(4 * kc + m, group, stride=4 * chunks), :] for kc in range(chunks)], 1)
        for r in range(4):
            values[4 * m + r] = v * at_ref[12 + r]
    i16 = iota((16, slots), 0).astype(F).astype(BF)
    i64 = iota((64, slots), 0).astype(F).astype(BF)
    zero = jnp.zeros((), BF)

    def spread(ref, i, s, n):
        row = jnp.broadcast_to(ref[i, pl.ds(s, 1), :], (16, slots)).astype(BF)
        return jnp.broadcast_to(row[None], (n // 16, 16, slots)).reshape(n, slots)

    def build(s):
        left = [None] * 16
        for r in range(4):
            here = i16 == spread(at_ref, r, s, 16)
            for m in range(4):
                left[4 * m + r] = jnp.where(here, spread(values, 4 * m + r, s, 16), zero)
        right = [jnp.where(i64 == spread(at_ref, 4 + r, s, 64), spread(at_ref, 8 + r, s, 64), zero) for r in range(4)]
        return jnp.concatenate(left, 0), jnp.concatenate(right, 0)

    for s in range(group):
        left, right = build(s)
        acc[...] += mm(left, right, ((1,), (1,)))


def project(values, at):
    tiles, slots = at.shape[1:]
    group = 32
    return pl.pallas_call(
        functools.partial(project_kernel, group, slots),
        grid=(tiles // group,),
        in_specs=[
            pl.BlockSpec((group * slots // 32, 128), lambda i: (i, 0)),
            pl.BlockSpec((16, group, slots), lambda i: (0, i, 0)),
        ],
        out_specs=pl.BlockSpec((256, 256), lambda i: (0, 0)),
        out_shape=struct(256, 256),
        scratch_shapes=[pltpu.VMEM((16, group, slots), F)],
        compiler_params=params(),
        name="project_rows",
    )(values, at)


def on_device(residual, counts, offsets, positions, coef_fine, coef_coarse, kappa_map, kappa_table, level_weight):
    tiles = residual.shape[2]
    packed = pack(counts, residual[0]).reshape(tiles, -1, 4, 128)
    values = lax.all_to_all(packed, AXES, split_axis=0, concat_axis=0, tiled=True).reshape(-1, 128)
    at = places(offsets[0], positions[0])
    fields = edges(coef_fine, coef_coarse, kappa_map, kappa_table, at)
    return tuple(finish(level_weight, project(values, at), fields))


def solution(mesh):
    rows = P(AXES, None, None, None)
    tile = P(None, "ty", "tx")
    return jax.shard_map(
        on_device,
        mesh=mesh,
        in_specs=(rows, P(AXES, None), rows, rows, tile, tile, P("ty", "tx"), P(), P()),
        out_specs=(tile, tile),
        check_vma=False,
    )
```

time: 68.7 us -> 60 us (0.87)
  the two profiles are of different devices: /device:TPU:39 before, /device:TPU:14 now
where the time goes in v2:
time: 60 us; the launch traced here: 59.7 us
  Pallas kernels  27.5 us (46%)
  starting transfers between devices  24.1 us (40%)
  waiting for transfers between devices  6.41 us (11%)
  local copies, waits for them, and re-layouts  0.89 us (1%)
  between operations  0.84 us (1%)
    pallas_call x1, Pallas kernels, project(): pl.pallas_call(functools.partial(project_kernel, group, slots), grid=(til...  15.8 us
    all_to_all x1, starting transfers between devices, on_device(): lax.all_to_all(packed, AXES, split_axis=0, concat_axis=0, tiled=True)  10.4 us
    ppermute x1, starting transfers between devices, edges(): from_left = lax.ppermute(to_right, 'tx', onward)  5.33 us
    pallas_call x1, Pallas kernels, places(): pl.pallas_call(place_kernel, grid=(tiles // group,), in_specs=[points, po...  5.05 us
    ppermute x1, starting transfers between devices, edges(): from_down = lax.ppermute(to_up, 'ty', back)  4.54 us
    ppermute x1, waiting for transfers between devices, edges(): from_left = lax.ppermute(to_right, 'tx', onward)  4.3 us
    pallas_call x1, Pallas kernels, pack(): pl.pallas_call(functools.partial(pack_kernel, block), in_specs=[pl.BlockS...  3.02 us
    pallas_call x1, Pallas kernels, finish(): pl.pallas_call(finish_kernel, in_specs=[pl.BlockSpec(memory_space=pltpu.S...  2.6 us
  transfers between devices with their start and end apart: 5, of which 2 were waited for; matrix products, arithmetic and copies ran while one was open for 0% of the time, Pallas kernels for 37%

profile of v2, /device:TPU:14, one launch (start us, length us, event | category | flops | bytes accessed | tf_op | source)
XLA Modules:
  0.0 59.7 jit_solution(10362458615569219885)
XLA Ops:
  0.6 3.0 %pack_rows.1 = f32[3072,128]{1,0:T(8,128)} custom-call(s32[1,128]{1,0:T(1,128)} %counts_ref.1, f32[4,128,768]{2,1,0:T(8,128)} %bitcast.9), custom_call_target="tpu_custom_call" | custom-call | tf_op jit(solution)/shard_map/pack_rows/pallas_call | solution.py:75
  3.7 0.0 copy-start
  3.7 0.0 copy-start.3
  3.7 0.0 copy-start.7
  3.7 0.0 copy-start.1
  3.7 0.0 copy-start.2
  3.7 10.4 %all-to-all-start = ((f32[128,6,4,128]{3,2,1,0:T(4,128)}), f32[128,6,4,128]{3,2,1,0:T(4,128)S(1)}, u32[]{:S(2)}, u32[]{:S(2)}) async-start(f32[128,6,4,128]{3,2,1,0:T(4,128)} %bitcast.8), calls=%async_computation | async-start | bytes 3145728 | tf_op jit(solution)/shard_map/all_to_all | solution.py:366
  14.1 0.0 copy-done
  14.1 0.0 copy-done.3
  14.1 0.0 copy-done.7
  14.1 0.0 copy-start.6
  14.1 0.8 %copy-done.6 = s32[128,128]{1,0:T(8,128)S(1)} copy-done((s32[128,128]{1,0:T(8,128)S(1)}, s32[128,128]{1,0:T(8,128)}, u32[]{:S(2)}) %copy-start.6) | copy-done | bytes 65560
  15.0 0.8 %edge_columns.1 = (f32[24,128]{1,0:T(8,128)S(1)}, f32[24,128]{1,0:T(8,128)S(1)}, f32[128,128]{1,0:T(8,128)S(1)}, f32[64,128]{1,0:T(8,128)S(1)}) custom-call(f32[2,8]{1,0:T(2,128)S(1)} %copy-done.7, f32[4,128,128]{2,1,0:T(8,128)S(1)} %copy-done, f32[4,64,64]{2,1,0:T(8,128)S(1)} %copy-done.3, s32[128,128]{1,0:T(8,128)S(1)} %copy-done.6), custom_call_target="tpu_custom_call" | custom-call | tf_op jit(solution)/shard_map/edge_columns/pallas_call | solution.py:219
  15.8 0.0 copy-start.4
  15.8 5.3 %collective-permute-start = (f32[24,128]{1,0:T(8,128)S(1)}, f32[24,128]{1,0:T(8,128)S(1)}, u32[]{:S(2)}, u32[]{:S(2)}) collective-permute-start(f32[24,128]{1,0:T(8,128)S(1)} %get-tuple-element.14), channel_id=1, source_target_pairs={{0,1},{1,2},{2,3},{3,4},{4,5},{5,6},{6,7},{8,9},{9,10},{10,11},{11... | collective-permute-start | bytes 36872 | tf_op jit(solution)/shard_map/ppermute | solution.py:228
  21.1 1.9 %collective-permute-start.1 = (f32[24,128]{1,0:T(8,128)S(1)}, f32[24,128]{1,0:T(8,128)S(1)}, u32[]{:S(2)}, u32[]{:S(2)}) collective-permute-start(f32[24,128]{1,0:T(8,128)S(1)} %get-tuple-element.15), channel_id=1, source_target_pairs={{1,0},{2,1},{3,2},{4,3},{5,4},{6,5},{7,6},{9,8},{10,9},{11,10},{12... | collective-permute-start | bytes 36872 | tf_op jit(solution)/shard_map/ppermute | solution.py:229
  23.0 0.0 copy-done.1
  23.0 0.0 copy-done.2
  23.0 5.1 %place_rows.1.at_ref = f32[16,128,768]{2,1,0:T(8,128)} custom-call(s32[2,128,768]{2,1,0:T(8,128)S(1)} %bitcast.6, f32[2,128,768]{2,1,0:T(8,128)S(1)} %bitcast.7), custom_call_target="tpu_custom_call" | custom-call | tf_op jit(solution)/shard_map/place_rows/pallas_call | solution.py:302
  28.1 4.3 %collective-permute-done.fl_ref = f32[24,128]{1,0:T(8,128)S(1)} collective-permute-done((f32[24,128]{1,0:T(8,128)S(1)}, f32[24,128]{1,0:T(8,128)S(1)}, u32[]{:S(2)}, u32[]{:S(2)}) %collective-permute-start) | collective-permute-done | bytes 12320 | tf_op jit(solution)/shard_map/ppermute | solution.py:228
  32.4 2.1 %collective-permute-done.1.fr_ref = f32[24,128]{1,0:T(8,128)S(1)} collective-permute-done((f32[24,128]{1,0:T(8,128)S(1)}, f32[24,128]{1,0:T(8,128)S(1)}, u32[]{:S(2)}, u32[]{:S(2)}) %collective-permute-start.1) | collective-permute-done | bytes 12320 | tf_op jit(solution)/shard_map/ppermute | solution.py:229
  34.5 0.0 copy-done.4
  34.5 0.3 edge_rows.1
  34.8 1.9 %collective-permute-start.2 = (f32[24,256]{1,0:T(8,128)S(1)}, f32[24,256]{1,0:T(8,128)S(1)}, u32[]{:S(2)}, u32[]{:S(2)}) collective-permute-start(f32[24,256]{1,0:T(8,128)S(1)} %get-tuple-element.20), channel_id=1, source_target_pairs={{0,8},{8,16},{16,24},{24,32},{32,40},{40,48},{48,56},{56,64},{64,7... | collective-permute-start | bytes 73736 | tf_op jit(solution)/shard_map/ppermute | solution.py:239
  36.7 4.5 %collective-permute-start.3 = (f32[24,256]{1,0:T(8,128)S(1)}, f32[24,256]{1,0:T(8,128)S(1)}, u32[]{:S(2)}, u32[]{:S(2)}) collective-permute-start(f32[24,256]{1,0:T(8,128)S(1)} %get-tuple-element.21), channel_id=1, source_target_pairs={{8,0},{16,8},{24,16},{32,24},{40,32},{48,40},{56,48},{64,56},{72,6... | collective-permute-start | bytes 73736 | tf_op jit(solution)/shard_map/ppermute | solution.py:240
  41.2 0.0 all-to-all-done
  41.3 0.0 copy-start.5
  41.3 0.0 copy-start.8
  41.3 15.8 %project_rows.1.acc = f32[256,256]{1,0:T(8,128)S(1)} custom-call(f32[3072,128]{1,0:T(8,128)S(1)} %bitcast.5, f32[16,128,768]{2,1,0:T(8,128)} %place_rows.1.at_ref), custom_call_target="tpu_custom_call" | custom-call | tf_op jit(solution)/shard_map/project_rows/pallas_call | solution.py:348
  57.1 0.0 collective-permute-done.2.fu_ref
  57.1 0.0 collective-permute-done.3.fd_ref
  57.1 2.6 %finish_tiles.1 = (f32[4,128,128]{2,1,0:T(8,128)}, f32[4,64,64]{2,1,0:T(8,128)}) custom-call(f32[2]{0:T(128)S(1)} %copy-done.8, f32[256,256]{1,0:T(8,128)S(1)} %project_rows.1.acc, f32[4,128,128]{2,1,0:T(8,128)S(1)} %copy-done, f32[4,128,128]{2,1,0:T(8,128)S(1)} %get-tuple-element.16.cs_ref, f32[4,64,128]{2,1,0:T(8,128)S(1)} %get-tuple-element.17.cm_ref, ...), custom_call_target="tpu_custom_call" | custom-call | tf_op jit(solution)/shard_map/finish_tiles/pallas_call | solution.py:246
  (2 shorter events, 0.0 us)
Async XLA Ops:
  3.7 10.4 %copy-start = (f32[4,128,128]{2,1,0:T(8,128)S(1)}, f32[4,128,128]{2,1,0:T(8,128)}, u32[]{:S(2)}) copy-start(f32[4,128,128]{2,1,0:T(8,128)} %cf_ref.5) | copy-start | bytes 786436
  3.7 10.4 %copy-start.3 = (f32[4,64,64]{2,1,0:T(8,128)S(1)}, f32[4,64,64]{2,1,0:T(8,128)}, u32[]{:S(2)}) copy-start(f32[4,64,64]{2,1,0:T(8,128)} %cc_ref.3) | copy-start | bytes 196612
  3.7 10.4 %copy-start.7 = (f32[2,8]{1,0:T(2,128)S(1)}, f32[2,8]{1,0:T(2,128)}, u32[]{:S(2)}) copy-start(f32[2,8]{1,0:T(2,128)} %table_ref.1) | copy-start | bytes 196
  3.7 19.3 %copy-start.1 = (s32[1,2,128,768]{3,2,1,0:T(8,128)S(1)}, s32[1,2,128,768]{3,2,1,0:T(8,128)}, u32[]{:S(2)}) copy-start(s32[1,2,128,768]{3,2,1,0:T(8,128)} %param.11) | copy-start | bytes 2359300
  3.7 19.3 %copy-start.2 = (f32[1,2,128,768]{3,2,1,0:T(8,128)S(1)}, f32[1,2,128,768]{3,2,1,0:T(8,128)}, u32[]{:S(2)}) copy-start(f32[1,2,128,768]{3,2,1,0:T(8,128)} %param.12) | copy-start | bytes 2359300
  3.7 37.5 %all-to-all-start = ((f32[128,6,4,128]{3,2,1,0:T(4,128)}), f32[128,6,4,128]{3,2,1,0:T(4,128)S(1)}, u32[]{:S(2)}, u32[]{:S(2)}) async-start(f32[128,6,4,128]{3,2,1,0:T(4,128)} %bitcast.8), calls=%async_computation | async-start | bytes 3145728 | tf_op jit(solution)/shard_map/all_to_all | solution.py:366
  14.1 0.8 %copy-start.6 = (s32[128,128]{1,0:T(8,128)S(1)}, s32[128,128]{1,0:T(8,128)}, u32[]{:S(2)}) copy-start(s32[128,128]{1,0:T(8,128)} %km_ref.1) | copy-start | bytes 196612
  15.8 18.7 %copy-start.4 = (f32[128,128]{1,0:T(8,128)}, f32[128,128]{1,0:T(8,128)S(1)}, u32[]{:S(2)}) copy-start(f32[128,128]{1,0:T(8,128)S(1)} %get-tuple-element.12.df_ref) | copy-start | bytes 196612
  15.8 16.6 %collective-permute-start = (f32[24,128]{1,0:T(8,128)S(1)}, f32[24,128]{1,0:T(8,128)S(1)}, u32[]{:S(2)}, u32[]{:S(2)}) collective-permute-start(f32[24,128]{1,0:T(8,128)S(1)} %get-tuple-element.14), channel_id=1, source_target_pairs={{0,1},{1,2},{2,3},{3,4},{4,5},{5,6},{6,7},{8,9},{9,10},{10,11},{11... | collective-permute-start | bytes 36872 | tf_op jit(solution)/shard_map/ppermute | solution.py:228
  21.1 13.4 %collective-permute-start.1 = (f32[24,128]{1,0:T(8,128)S(1)}, f32[24,128]{1,0:T(8,128)S(1)}, u32[]{:S(2)}, u32[]{:S(2)}) collective-permute-start(f32[24,128]{1,0:T(8,128)S(1)} %get-tuple-element.15), channel_id=1, source_target_pairs={{1,0},{2,1},{3,2},{4,3},{5,4},{6,5},{7,6},{9,8},{10,9},{11,10},{12... | collective-permute-start | bytes 36872 | tf_op jit(solution)/shard_map/ppermute | solution.py:229
  34.8 22.3 %collective-permute-start.2 = (f32[24,256]{1,0:T(8,128)S(1)}, f32[24,256]{1,0:T(8,128)S(1)}, u32[]{:S(2)}, u32[]{:S(2)}) collective-permute-start(f32[24,256]{1,0:T(8,128)S(1)} %get-tuple-element.20), channel_id=1, source_target_pairs={{0,8},{8,16},{16,24},{24,32},{32,40},{40,48},{48,56},{56,64},{64,7... | collective-permute-start | bytes 73736 | tf_op jit(solution)/shard_map/ppermute | solution.py:239
  36.7 20.4 %collective-permute-start.3 = (f32[24,256]{1,0:T(8,128)S(1)}, f32[24,256]{1,0:T(8,128)S(1)}, u32[]{:S(2)}, u32[]{:S(2)}) collective-permute-start(f32[24,256]{1,0:T(8,128)S(1)} %get-tuple-element.21), channel_id=1, source_target_pairs={{8,0},{16,8},{24,16},{32,24},{40,32},{48,40},{56,48},{64,56},{72,6... | collective-permute-start | bytes 73736 | tf_op jit(solution)/shard_map/ppermute | solution.py:240
  41.3 15.9 %copy-start.5 = (f32[128,128]{1,0:T(8,128)S(1)}, f32[128,128]{1,0:T(8,128)}, u32[]{:S(2)}) copy-start(f32[128,128]{1,0:T(8,128)} %copy-done.4) | copy-start | bytes 196612
  41.3 15.9 %copy-start.8 = (f32[2]{0:T(128)S(1)}, f32[2]{0:T(128)}, u32[]{:S(2)}) copy-start(f32[2]{0:T(128)} %lw_ref.1) | copy-start | bytes 28

commit v3 on v2

--- a/solution.py
+++ b/solution.py
@@ -37,23 +37,26 @@
     return pltpu.CompilerParams(vmem_limit_bytes=VMEM_LIMIT)
 
 
-def pack_kernel(block, counts_ref, res_ref, out_ref, loaded, built, sems, out_sems):
+def pack_kernel(block, counts_ref, res_ref, out_ref, counts, loaded, built, sems, out_sems, count_sem):
     tiles, slots = res_ref.shape[1:]
     parts = tiles // block
     chunks = slots // 128
     rows = 4 * chunks * block
+    take = pltpu.make_async_copy(counts_ref, counts, count_sem)
+    take.start()
     loads = [
         pltpu.make_async_copy(res_ref.at[:, pl.ds(i * block, block), :], loaded.at[i], sems.at[i]) for i in range(parts)
     ]
     for load in loads:
         load.start()
+    take.wait()
     stores = []
     for i in range(parts):
         loads[i].wait()
         for d in range(0, block, 8):
             live = jnp.zeros((8, 128), jnp.int32)
             for j in range(8):
-                live = jnp.where(iota((8, 128), 0) == j, counts_ref[0, i * block + d + j], live)
+                live = jnp.where(iota((8, 128), 0) == j, counts[0, i * block + d + j], live)
             for kc in range(chunks):
                 keep = iota((8, 128), 1) + 128 * kc < live
                 for m in range(4):
@@ -69,19 +72,21 @@
 
 def pack(counts, residual):
     channels, tiles, slots = residual.shape
-    block = 16
+    block = 32
     parts = tiles // block
     rows = 4 * (slots // 128)
     return pl.pallas_call(
         functools.partial(pack_kernel, block),
-        in_specs=[pl.BlockSpec(memory_space=pltpu.SMEM), pl.BlockSpec(memory_space=pltpu.HBM)],
+        in_specs=[pl.BlockSpec(memory_space=pltpu.HBM)] * 2,
         out_specs=pl.BlockSpec(memory_space=pl.ANY),
         out_shape=struct(tiles * rows, 128),
         scratch_shapes=[
+            pltpu.SMEM((1, tiles), jnp.int32),
             pltpu.VMEM((parts, channels, block, slots), F),
             pltpu.VMEM((parts, block * rows, 128), F),
             pltpu.SemaphoreType.DMA((parts,)),
             pltpu.SemaphoreType.DMA((parts,)),
+            pltpu.SemaphoreType.DMA,
         ],
         compiler_params=pltpu.CompilerParams(vmem_limit_bytes=62 * 1024 * 1024),
         name="pack_rows",
@@ -151,37 +156,12 @@
     send(17, 0, dm_ref[...], 64, 1)
 
 
-def finish_kernel(lw_ref, acc, cf_ref, cs_ref, cm_ref, df_ref, ds_ref, dm_ref, fu_ref, fd_ref, fine_ref, coarse_ref, vf, wf, vc, wc, tall, low):
-    def apply(field, diag):
-        rows, lanes = field.shape
-        near = pltpu.roll(field, 1, 0) + pltpu.roll(field, rows - 1, 0)
-        near = near + (pltpu.roll(field, 1, 1) + pltpu.roll(field, lanes - 1, 1))
-        return diag * field - near
-
-    def twice(field, diag):
-        first = jnp.where(diag > 0.0, apply(field, diag), 0.0)
-        return apply(first, diag)
-
-    def rim(scratch, size, row, width, lanes):
-        last = scratch.shape[0]
-        scratch[size:last, :] = jnp.zeros((last - size, lanes), F)
-        scratch[size:size + width, :] = fd_ref[row:row + width, 0:lanes]
-        scratch[last - width:last, :] = fu_ref[row:row + width, 0:lanes]
-
-    wf[0:128, 0:128] = df_ref[...]
-    wf[0:128, 128:256] = ds_ref[...]
-    rim(wf, 128, 16, 1, 256)
-    wc[0:64, :] = dm_ref[...]
-    rim(wc, 64, 17, 1, 128)
-    for m in range(4):
-        vf[0:128, 0:128] = cf_ref[m]
-        vf[0:128, 128:256] = cs_ref[m]
-        rim(vf, 128, 2 * m, 2, 256)
-        fine_ref[m] = twice(vf[...], wf[...])[0:128, 0:128]
-        vc[0:64, :] = cm_ref[m]
-        rim(vc, 64, 8 + 2 * m, 2, 128)
-        coarse_ref[m] = twice(vc[...], wc[...])[0:64, 0:64]
-
+def finish_kernel(
+    lw_ref, acc, cf_ref, cs_ref, cm_ref, df_ref, ds_ref, dm_ref, fu_ref, fd_ref, fine_ref, coarse_ref,
+    lw, vf, wf, vc, wc, tall, low, fine_out, coarse_out, sems, lw_sem,
+):
+    take = pltpu.make_async_copy(lw_ref, lw, lw_sem)
+    take.start()
     a = iota((256, 256), 0)
     b = iota((256, 256), 1)
     place = ((b >> 7) == ((a >> 5) & 1)) & ((b & 127) == 1 + 4 * (a & 31) + (a >> 6))
@@ -189,6 +169,36 @@
     wide = sum(mm(p, place) for p in split3(acc[...]))
     far = jnp.abs(iota((128, 128), 0) - 2 * iota((128, 128), 1))
     halve = jnp.where(far == 0, 0.75, jnp.where(far == 1, 0.5, jnp.where(far == 2, 0.125, 0.0))).astype(BF)
+
+    def apply(field, diag):
+        rows, lanes = field.shape
+        near = pltpu.roll(field, 1, 0) + pltpu.roll(field, rows - 1, 0)
+        near = near + (pltpu.roll(field, 1, 1) + pltpu.roll(field, lanes - 1, 1))
+        return diag * field - near
+
+    def twice(field, diag):
+        first = jnp.where(diag > 0.0, apply(field, diag), 0.0)
+        return apply(first, diag)
+
+    def rim(scratch, size, row, width, lanes):
+        last = scratch.shape[0]
+        scratch[size:last, :] = jnp.zeros((last - size, lanes), F)
+        scratch[size:size + width, :] = fd_ref[row:row + width, 0:lanes]
+        scratch[last - width:last, :] = fu_ref[row:row + width, 0:lanes]
+
+    wf[0:128, 0:128] = df_ref[...]
+    wf[0:128, 128:256] = ds_ref[...]
+    rim(wf, 128, 16, 1, 256)
+    wc[0:64, :] = dm_ref[...]
+    rim(wc, 64, 17, 1, 128)
+    for m in range(4):
+        vf[m, 0:128, 0:128] = cf_ref[m]
+        vf[m, 0:128, 128:256] = cs_ref[m]
+        rim(vf.at[m], 128, 2 * m, 2, 256)
+        vc[m, 0:64, :] = cm_ref[m]
+        rim(vc.at[m], 64, 8 + 2 * m, 2, 128)
+    take.wait()
+    sends = []
     for m in range(4):
         tall[m, 0:16, :] = jnp.zeros((16, 128), F)
         tall[m, 72:144, :] = jnp.zeros((72, 128), F)
@@ -198,12 +208,19 @@
                 spots = pl.ds(9 + 61 * h + r, 16, stride=4)
                 part = wide[at:at + 16, h * 128:(h + 1) * 128]
                 tall[m, spots, :] = part if h == 0 else part + tall[m, spots, :]
-        fine_ref[m] = lw_ref[0] * tall[m, 8:136, :] - fine_ref[m]
         every = [tall[m, pl.ds(8 + k, 64, stride=2), :] for k in range(-2, 3)]
         low[m * 64:(m + 1) * 64, :] = 0.75 * every[2] + 0.5 * (every[1] + every[3]) + 0.125 * (every[0] + every[4])
+        fine_out[m] = lw[0] * tall[m, 8:136, :] - twice(vf[m], wf[...])[0:128, 0:128]
+        send = pltpu.make_async_copy(fine_out.at[m], fine_ref.at[m], sems.at[m])
+        send.start()
+        sends.append(send)
     coarse = sum(mm(p, halve) for p in split3(low[...]))
     for m in range(4):
-        coarse_ref[m] = lw_ref[1] * coarse[m * 64:(m + 1) * 64, 0:64] - coarse_ref[m]
+        coarse_out[m] = lw[1] * coarse[m * 64:(m + 1) * 64, 0:64] - twice(vc[m], wc[...])[0:64, 0:64]
+    send = pltpu.make_async_copy(coarse_out, coarse_ref, sems.at[4])
+    send.start()
+    for send in sends + [send]:
+        send.wait()
 
 
 def neighbours(axis):
@@ -245,15 +262,21 @@
     vmem = pl.BlockSpec(memory_space=pltpu.VMEM)
     return pl.pallas_call(
         finish_kernel,
-        in_specs=[pl.BlockSpec(memory_space=pltpu.SMEM)] + [vmem] * (1 + len(fields)),
+        in_specs=[pl.BlockSpec(memory_space=pl.ANY)] + [vmem] * (1 + len(fields)),
+        out_specs=[pl.BlockSpec(memory_space=pl.ANY)] * 2,
         out_shape=[struct(4, 128, 128), struct(4, 64, 64)],
         scratch_shapes=[
+            pltpu.SMEM((2,), F),
+            pltpu.VMEM((4, 136, 256), F),
             pltpu.VMEM((136, 256), F),
-            pltpu.VMEM((136, 256), F),
-            pltpu.VMEM((72, 128), F),
+            pltpu.VMEM((4, 72, 128), F),
             pltpu.VMEM((72, 128), F),
             pltpu.VMEM((4, 144, 128), F),
             pltpu.VMEM((256, 128), F),
+            pltpu.VMEM((4, 128, 128), F),
+            pltpu.VMEM((4, 64, 64), F),
+            pltpu.SemaphoreType.DMA((5,)),
+            pltpu.SemaphoreType.DMA,
         ],
         compiler_params=params(),
         name="finish_tiles",

time: 60 us -> 59.2 us (0.987)
  Pallas kernels: 27.5 us -> 26.7 us
    pallas_call x1, Pallas kernels: 3.02 us -> 2.3 us  [pack(): pl.pallas_call(functools.partial(pack_kernel, block), in_specs=[pl.BlockS...]
where the time goes in v3:
time: 59.2 us; the launch traced here: 58.9 us
  Pallas kernels  26.7 us (45%)
  starting transfers between devices  24.1 us (41%)
  waiting for transfers between devices  6.41 us (11%)
  local copies, waits for them, and re-layouts  0.89 us (2%)
  between operations  0.84 us (1%)
    pallas_call x1, Pallas kernels, project(): pl.pallas_call(functools.partial(project_kernel, group, slots), grid=(til...  15.8 us
    all_to_all x1, starting transfers between devices, on_device(): lax.all_to_all(packed, AXES, split_axis=0, concat_axis=0, tiled=True)  10.4 us
    ppermute x1, starting transfers between devices, edges(): from_left = lax.ppermute(to_right, 'tx', onward)  5.33 us
    pallas_call x1, Pallas kernels, places(): pl.pallas_call(place_kernel, grid=(tiles // group,), in_specs=[points, po...  5.05 us
    ppermute x1, starting transfers between devices, edges(): from_down = lax.ppermute(to_up, 'ty', back)  4.54 us
    ppermute x1, waiting for transfers between devices, edges(): from_left = lax.ppermute(to_right, 'tx', onward)  4.3 us
    pallas_call x1, Pallas kernels, finish(): pl.pallas_call(finish_kernel, in_specs=[pl.BlockSpec(memory_space=pl.ANY)...  2.47 us
    pallas_call x1, Pallas kernels, pack(): pl.pallas_call(functools.partial(pack_kernel, block), in_specs=[pl.BlockS...  2.3 us
  transfers between devices with their start and end apart: 5, of which 2 were waited for; matrix products, arithmetic and copies ran while one was open for 0% of the time, Pallas kernels for 37%

profile of v3, /device:TPU:14, one launch (start us, length us, event | category | flops | bytes accessed | tf_op | source)
XLA Modules:
  0.0 58.9 jit_solution(6317604524964916495)
XLA Ops:
  0.6 2.3 %pack_rows.1 = f32[3072,128]{1,0:T(8,128)} custom-call(s32[1,128]{1,0:T(1,128)} %counts_ref.1, f32[4,128,768]{2,1,0:T(8,128)} %bitcast.9), custom_call_target="tpu_custom_call" | custom-call | tf_op jit(solution)/shard_map/pack_rows/pallas_call | solution.py:78
  2.9 0.0 copy-start
  2.9 0.0 copy-start.3
  3.0 0.0 copy-start.7
  3.0 0.0 copy-start.1
  3.0 0.0 copy-start.2
  3.0 10.4 %all-to-all-start = ((f32[128,6,4,128]{3,2,1,0:T(4,128)}), f32[128,6,4,128]{3,2,1,0:T(4,128)S(1)}, u32[]{:S(2)}, u32[]{:S(2)}) async-start(f32[128,6,4,128]{3,2,1,0:T(4,128)} %bitcast.8), calls=%async_computation | async-start | bytes 3145728 | tf_op jit(solution)/shard_map/all_to_all | solution.py:389
  13.4 0.0 copy-done
  13.4 0.0 copy-done.3
  13.4 0.0 copy-done.7
  13.4 0.0 copy-start.6
  13.4 0.8 %copy-done.6 = s32[128,128]{1,0:T(8,128)S(1)} copy-done((s32[128,128]{1,0:T(8,128)S(1)}, s32[128,128]{1,0:T(8,128)}, u32[]{:S(2)}) %copy-start.6) | copy-done | bytes 65560
  14.2 0.8 %edge_columns.1 = (f32[24,128]{1,0:T(8,128)S(1)}, f32[24,128]{1,0:T(8,128)S(1)}, f32[128,128]{1,0:T(8,128)S(1)}, f32[64,128]{1,0:T(8,128)S(1)}) custom-call(f32[2,8]{1,0:T(2,128)S(1)} %copy-done.7, f32[4,128,128]{2,1,0:T(8,128)S(1)} %copy-done, f32[4,64,64]{2,1,0:T(8,128)S(1)} %copy-done.3, s32[128,128]{1,0:T(8,128)S(1)} %copy-done.6), custom_call_target="tpu_custom_call" | custom-call | tf_op jit(solution)/shard_map/edge_columns/pallas_call | solution.py:236
  15.0 0.0 copy-start.4
  15.0 5.3 %collective-permute-start = (f32[24,128]{1,0:T(8,128)S(1)}, f32[24,128]{1,0:T(8,128)S(1)}, u32[]{:S(2)}, u32[]{:S(2)}) collective-permute-start(f32[24,128]{1,0:T(8,128)S(1)} %get-tuple-element.14), channel_id=1, source_target_pairs={{0,1},{1,2},{2,3},{3,4},{4,5},{5,6},{6,7},{8,9},{9,10},{10,11},{11... | collective-permute-start | bytes 36872 | tf_op jit(solution)/shard_map/ppermute | solution.py:245
  20.4 1.9 %collective-permute-start.1 = (f32[24,128]{1,0:T(8,128)S(1)}, f32[24,128]{1,0:T(8,128)S(1)}, u32[]{:S(2)}, u32[]{:S(2)}) collective-permute-start(f32[24,128]{1,0:T(8,128)S(1)} %get-tuple-element.15), channel_id=1, source_target_pairs={{1,0},{2,1},{3,2},{4,3},{5,4},{6,5},{7,6},{9,8},{10,9},{11,10},{12... | collective-permute-start | bytes 36872 | tf_op jit(solution)/shard_map/ppermute | solution.py:246
  22.3 0.0 copy-done.1
  22.3 0.0 copy-done.2
  22.3 5.1 %place_rows.1.at_ref = f32[16,128,768]{2,1,0:T(8,128)} custom-call(s32[2,128,768]{2,1,0:T(8,128)S(1)} %bitcast.6, f32[2,128,768]{2,1,0:T(8,128)S(1)} %bitcast.7), custom_call_target="tpu_custom_call" | custom-call | tf_op jit(solution)/shard_map/place_rows/pallas_call | solution.py:325
  27.4 4.3 %collective-permute-done.fl_ref = f32[24,128]{1,0:T(8,128)S(1)} collective-permute-done((f32[24,128]{1,0:T(8,128)S(1)}, f32[24,128]{1,0:T(8,128)S(1)}, u32[]{:S(2)}, u32[]{:S(2)}) %collective-permute-start) | collective-permute-done | bytes 12320 | tf_op jit(solution)/shard_map/ppermute | solution.py:245
  31.7 2.1 %collective-permute-done.1.fr_ref = f32[24,128]{1,0:T(8,128)S(1)} collective-permute-done((f32[24,128]{1,0:T(8,128)S(1)}, f32[24,128]{1,0:T(8,128)S(1)}, u32[]{:S(2)}, u32[]{:S(2)}) %collective-permute-start.1) | collective-permute-done | bytes 12320 | tf_op jit(solution)/shard_map/ppermute | solution.py:246
  33.8 0.0 copy-done.4
  33.8 0.3 edge_rows.1
  34.0 1.9 %collective-permute-start.2 = (f32[24,256]{1,0:T(8,128)S(1)}, f32[24,256]{1,0:T(8,128)S(1)}, u32[]{:S(2)}, u32[]{:S(2)}) collective-permute-start(f32[24,256]{1,0:T(8,128)S(1)} %get-tuple-element.20), channel_id=1, source_target_pairs={{0,8},{8,16},{16,24},{24,32},{32,40},{40,48},{48,56},{56,64},{64,7... | collective-permute-start | bytes 73736 | tf_op jit(solution)/shard_map/ppermute | solution.py:256
  36.0 4.5 %collective-permute-start.3 = (f32[24,256]{1,0:T(8,128)S(1)}, f32[24,256]{1,0:T(8,128)S(1)}, u32[]{:S(2)}, u32[]{:S(2)}) collective-permute-start(f32[24,256]{1,0:T(8,128)S(1)} %get-tuple-element.21), channel_id=1, source_target_pairs={{8,0},{16,8},{24,16},{32,24},{40,32},{48,40},{56,48},{64,56},{72,6... | collective-permute-start | bytes 73736 | tf_op jit(solution)/shard_map/ppermute | solution.py:257
  40.5 0.0 all-to-all-done
  40.5 0.0 copy-start.5
  40.5 0.0 copy-start.8
  40.6 15.8 %project_rows.1.acc = f32[256,256]{1,0:T(8,128)S(1)} custom-call(f32[3072,128]{1,0:T(8,128)S(1)} %bitcast.5, f32[16,128,768]{2,1,0:T(8,128)} %place_rows.1.at_ref), custom_call_target="tpu_custom_call" | custom-call | tf_op jit(solution)/shard_map/project_rows/pallas_call | solution.py:371
  56.4 0.0 collective-permute-done.2.fu_ref
  56.4 0.0 collective-permute-done.3.fd_ref
  56.4 2.5 %finish_tiles.1 = (f32[4,128,128]{2,1,0:T(8,128)}, f32[4,64,64]{2,1,0:T(8,128)}) custom-call(f32[2]{0:T(128)S(1)} %copy-done.8, f32[256,256]{1,0:T(8,128)S(1)} %project_rows.1.acc, f32[4,128,128]{2,1,0:T(8,128)S(1)} %copy-done, f32[4,128,128]{2,1,0:T(8,128)S(1)} %get-tuple-element.16.cs_ref, f32[4,64,128]{2,1,0:T(8,128)S(1)} %get-tuple-element.17.cm_ref, ...), custom_call_target="tpu_custom_call" | custom-call | tf_op jit(solution)/shard_map/finish_tiles/pallas_call | solution.py:263
  (2 shorter events, 0.0 us)
Async XLA Ops:
  2.9 10.4 %copy-start = (f32[4,128,128]{2,1,0:T(8,128)S(1)}, f32[4,128,128]{2,1,0:T(8,128)}, u32[]{:S(2)}) copy-start(f32[4,128,128]{2,1,0:T(8,128)} %cf_ref.5) | copy-start | bytes 786436
  2.9 10.4 %copy-start.3 = (f32[4,64,64]{2,1,0:T(8,128)S(1)}, f32[4,64,64]{2,1,0:T(8,128)}, u32[]{:S(2)}) copy-start(f32[4,64,64]{2,1,0:T(8,128)} %cc_ref.3) | copy-start | bytes 196612
  3.0 10.4 %copy-start.7 = (f32[2,8]{1,0:T(2,128)S(1)}, f32[2,8]{1,0:T(2,128)}, u32[]{:S(2)}) copy-start(f32[2,8]{1,0:T(2,128)} %table_ref.1) | copy-start | bytes 196
  3.0 19.3 %copy-start.1 = (s32[1,2,128,768]{3,2,1,0:T(8,128)S(1)}, s32[1,2,128,768]{3,2,1,0:T(8,128)}, u32[]{:S(2)}) copy-start(s32[1,2,128,768]{3,2,1,0:T(8,128)} %param.11) | copy-start | bytes 2359300
  3.0 19.3 %copy-start.2 = (f32[1,2,128,768]{3,2,1,0:T(8,128)S(1)}, f32[1,2,128,768]{3,2,1,0:T(8,128)}, u32[]{:S(2)}) copy-start(f32[1,2,128,768]{3,2,1,0:T(8,128)} %param.12) | copy-start | bytes 2359300
  3.0 37.5 %all-to-all-start = ((f32[128,6,4,128]{3,2,1,0:T(4,128)}), f32[128,6,4,128]{3,2,1,0:T(4,128)S(1)}, u32[]{:S(2)}, u32[]{:S(2)}) async-start(f32[128,6,4,128]{3,2,1,0:T(4,128)} %bitcast.8), calls=%async_computation | async-start | bytes 3145728 | tf_op jit(solution)/shard_map/all_to_all | solution.py:389
  13.4 0.8 %copy-start.6 = (s32[128,128]{1,0:T(8,128)S(1)}, s32[128,128]{1,0:T(8,128)}, u32[]{:S(2)}) copy-start(s32[128,128]{1,0:T(8,128)} %km_ref.1) | copy-start | bytes 196612
  15.0 18.7 %copy-start.4 = (f32[128,128]{1,0:T(8,128)}, f32[128,128]{1,0:T(8,128)S(1)}, u32[]{:S(2)}) copy-start(f32[128,128]{1,0:T(8,128)S(1)} %get-tuple-element.12.df_ref) | copy-start | bytes 196612
  15.0 16.6 %collective-permute-start = (f32[24,128]{1,0:T(8,128)S(1)}, f32[24,128]{1,0:T(8,128)S(1)}, u32[]{:S(2)}, u32[]{:S(2)}) collective-permute-start(f32[24,128]{1,0:T(8,128)S(1)} %get-tuple-element.14), channel_id=1, source_target_pairs={{0,1},{1,2},{2,3},{3,4},{4,5},{5,6},{6,7},{8,9},{9,10},{10,11},{11... | collective-permute-start | bytes 36872 | tf_op jit(solution)/shard_map/ppermute | solution.py:245
  20.4 13.4 %collective-permute-start.1 = (f32[24,128]{1,0:T(8,128)S(1)}, f32[24,128]{1,0:T(8,128)S(1)}, u32[]{:S(2)}, u32[]{:S(2)}) collective-permute-start(f32[24,128]{1,0:T(8,128)S(1)} %get-tuple-element.15), channel_id=1, source_target_pairs={{1,0},{2,1},{3,2},{4,3},{5,4},{6,5},{7,6},{9,8},{10,9},{11,10},{12... | collective-permute-start | bytes 36872 | tf_op jit(solution)/shard_map/ppermute | solution.py:246
  34.0 22.3 %collective-permute-start.2 = (f32[24,256]{1,0:T(8,128)S(1)}, f32[24,256]{1,0:T(8,128)S(1)}, u32[]{:S(2)}, u32[]{:S(2)}) collective-permute-start(f32[24,256]{1,0:T(8,128)S(1)} %get-tuple-element.20), channel_id=1, source_target_pairs={{0,8},{8,16},{16,24},{24,32},{32,40},{40,48},{48,56},{56,64},{64,7... | collective-permute-start | bytes 73736 | tf_op jit(solution)/shard_map/ppermute | solution.py:256
  36.0 20.4 %collective-permute-start.3 = (f32[24,256]{1,0:T(8,128)S(1)}, f32[24,256]{1,0:T(8,128)S(1)}, u32[]{:S(2)}, u32[]{:S(2)}) collective-permute-start(f32[24,256]{1,0:T(8,128)S(1)} %get-tuple-element.21), channel_id=1, source_target_pairs={{8,0},{16,8},{24,16},{32,24},{40,32},{48,40},{56,48},{64,56},{72,6... | collective-permute-start | bytes 73736 | tf_op jit(solution)/shard_map/ppermute | solution.py:257
  40.5 15.9 %copy-start.5 = (f32[128,128]{1,0:T(8,128)S(1)}, f32[128,128]{1,0:T(8,128)}, u32[]{:S(2)}) copy-start(f32[128,128]{1,0:T(8,128)} %copy-done.4) | copy-start | bytes 196612
  40.5 15.9 %copy-start.8 = (f32[2]{0:T(128)S(1)}, f32[2]{0:T(128)}, u32[]{:S(2)}) copy-start(f32[2]{0:T(128)} %lw_ref.1) | copy-start | bytes 28

commit v4 on v3

--- a/solution.py
+++ b/solution.py
@@ -100,9 +100,14 @@
     return 4.0 + total
 
 
-def columns_kernel(table_ref, cf_ref, cc_ref, km_ref, left_ref, right_ref, df_ref, dc_ref, square):
-    left_ref[...] = jnp.zeros_like(left_ref)
-    right_ref[...] = jnp.zeros_like(right_ref)
+def is_odd(axis):
+    return (lax.axis_index(axis) & 1) == 1
+
+
+def columns_kernel(table_ref, cf_ref, cc_ref, km_ref, with_ref, off_ref, df_ref, dc_ref, square):
+    odd = is_odd("tx")
+    with_ref[...] = jnp.zeros_like(with_ref)
+    off_ref[...] = jnp.zeros_like(off_ref)
     square[...] = jnp.zeros_like(square)
     df = classes_to_diag(km_ref[...], table_ref, 0)
     df_ref[...] = df
@@ -113,8 +118,9 @@
     dc_ref[...] = dc
 
     def send(row, turned, size, width):
-        left_ref[pl.ds(row, width), :] = turned[0:width]
-        right_ref[pl.ds(row, width), :] = turned[size - width:size]
+        low, high = turned[0:width], turned[size - width:size]
+        with_ref[pl.ds(row, width), :] = jnp.where(odd, low, high)
+        off_ref[pl.ds(row, width), :] = jnp.where(odd, high, low)
 
     for m in range(4):
         send(2 * m, cf_ref[m].T, 128, 2)
@@ -125,40 +131,76 @@
     send(17, square[...].T, 64, 1)
 
 
-def rows_kernel(cf_ref, cc_ref, df_ref, dc_ref, fl_ref, fr_ref, at_ref, up_ref, down_ref, cs_ref, cm_ref, ds_ref, dm_ref, square):
-    up_ref[...] = jnp.zeros_like(up_ref)
-    down_ref[...] = jnp.zeros_like(down_ref)
+def cross(field):
+    rows, lanes = field.shape
+    near = pltpu.roll(field, 1, 1) + pltpu.roll(field, lanes - 1, 1)
+    return near + (pltpu.roll(field, 1, 0) + pltpu.roll(field, rows - 1, 0))
+
+
+def rows_kernel(
+    cf_ref, cc_ref, df_ref, dc_ref, fw_ref, fo_ref, at_ref, with_ref, off_ref, bf_ref, bc_ref, square, vf, wf, vc, wc
+):
+    odd_x, odd_y = is_odd("tx"), is_odd("ty")
+    with_ref[...] = jnp.zeros_like(with_ref)
+    off_ref[...] = jnp.zeros_like(off_ref)
+    left = jnp.where(odd_x, fw_ref[...], fo_ref[...])
+    right = jnp.where(odd_x, fo_ref[...], fw_ref[...])
 
     def sides(row, first, width):
         square[...] = jnp.zeros_like(square)
-        square[first:first + width, :] = fr_ref[row:row + width, :]
-        square[128 - width:128, :] = fl_ref[row:row + width, :]
+        square[first:first + width, :] = right[row:row + width, :]
+        square[128 - width:128, :] = left[row:row + width, :]
         return square[...].T
 
-    def send(row, lane, field, size, width):
-        lanes = pl.ds(lane, 128)
-        up_ref[pl.ds(row, width), lanes] = field[0:width]
-        down_ref[pl.ds(row, width), lanes] = field[size - width:size]
-
-    for m in range(4):
-        side = sides(2 * m, 0, 2)
-        cs_ref[m] = side
-        send(2 * m, 0, cf_ref[m], 128, 2)
-        send(2 * m, 128, side, 128, 2)
-        cm_ref[m] = sides(8 + 2 * m, 64, 2)[0:64]
-        cm_ref[m, :, 0:64] = cc_ref[m]
-        send(8 + 2 * m, 0, cm_ref[m], 64, 2)
-    side = sides(16, 0, 1)
-    ds_ref[...] = side
-    send(16, 0, df_ref[...], 128, 1)
-    send(16, 128, side, 128, 1)
-    dm_ref[...] = dc_ref[...] + sides(17, 64, 1)[0:64]
-    send(17, 0, dm_ref[...], 64, 1)
+    def send(row, field, size, width):
+        lanes = field.shape[1]
+        low, high = field[0:width], field[size - width:size]
+        with_ref[pl.ds(row, width), 0:lanes] = jnp.where(odd_y, low, high)
+        off_ref[pl.ds(row, width), 0:lanes] = jnp.where(odd_y, high, low)
+
+    def twice(field, diag):
+        first = jnp.where(diag > 0.0, diag * field - cross(field), 0.0)
+        return diag * first - cross(first)
+
+    wf[...] = jnp.zeros_like(wf)
+    wf[0:128, 0:128] = df_ref[...]
+    wf[0:128, 128:256] = sides(16, 0, 1)
+    send(16, wf[...], 128, 1)
+    wc[...] = jnp.zeros_like(wc)
+    wc[0:64, :] = dc_ref[...] + sides(17, 64, 1)[0:64]
+    send(17, wc[...], 64, 1)
+    for m in range(4):
+        vf[m, 128:136, :] = jnp.zeros((8, 256), F)
+        vf[m, 0:128, 0:128] = cf_ref[m]
+        vf[m, 0:128, 128:256] = sides(2 * m, 0, 2)
+        send(2 * m, vf[m], 128, 2)
+        vc[m, 64:72, :] = jnp.zeros((8, 128), F)
+        vc[m, 0:64, :] = sides(8 + 2 * m, 64, 2)[0:64]
+        vc[m, 0:64, 0:64] = cc_ref[m]
+        send(8 + 2 * m, vc[m], 64, 2)
+    for m in range(4):
+        bf_ref[m] = twice(vf[m], wf[...])[0:128, 0:128]
+        bc_ref[m] = twice(vc[m], wc[...])[0:64, :]
+
+
+def rim(own, other, rows, diag, lanes, step):
+    here = own[diag:diag + 1, 0:lanes]
+    there = other[diag:diag + 1, 0:lanes]
+    near = other[rows:rows + 8, 0:lanes]
+    far = pltpu.roll(near, step, 0)
+    edge = pltpu.roll(own[rows:rows + 8, 0:lanes], step, 0)
+
+    def sideways(x):
+        return pltpu.roll(x, 1, 1) + pltpu.roll(x, lanes - 1, 1)
+
+    change = jnp.where(here > 0.0, -near, 0.0)
+    beyond = jnp.where(there > 0.0, there * near - (far + edge + sideways(near)), 0.0)
+    return here * change - sideways(change) - beyond, -change
 
 
 def finish_kernel(
-    lw_ref, acc, cf_ref, cs_ref, cm_ref, df_ref, ds_ref, dm_ref, fu_ref, fd_ref, fine_ref, coarse_ref,
-    lw, vf, wf, vc, wc, tall, low, fine_out, coarse_out, sems, lw_sem,
+    lw_ref, acc, bf_ref, bc_ref, with_ref, off_ref, fw_ref, fo_ref, fine_ref, coarse_ref,
+    lw, tall, low, fine_out, coarse_out, sems, lw_sem,
 ):
     take = pltpu.make_async_copy(lw_ref, lw, lw_sem)
     take.start()
@@ -170,33 +212,21 @@
     far = jnp.abs(iota((128, 128), 0) - 2 * iota((128, 128), 1))
     halve = jnp.where(far == 0, 0.75, jnp.where(far == 1, 0.5, jnp.where(far == 2, 0.125, 0.0))).astype(BF)
 
-    def apply(field, diag):
-        rows, lanes = field.shape
-        near = pltpu.roll(field, 1, 0) + pltpu.roll(field, rows - 1, 0)
-        near = near + (pltpu.roll(field, 1, 1) + pltpu.roll(field, lanes - 1, 1))
-        return diag * field - near
-
-    def twice(field, diag):
-        first = jnp.where(diag > 0.0, apply(field, diag), 0.0)
-        return apply(first, diag)
-
-    def rim(scratch, size, row, width, lanes):
-        last = scratch.shape[0]
-        scratch[size:last, :] = jnp.zeros((last - size, lanes), F)
-        scratch[size:size + width, :] = fd_ref[row:row + width, 0:lanes]
-        scratch[last - width:last, :] = fu_ref[row:row + width, 0:lanes]
-
-    wf[0:128, 0:128] = df_ref[...]
-    wf[0:128, 128:256] = ds_ref[...]
-    rim(wf, 128, 16, 1, 256)
-    wc[0:64, :] = dm_ref[...]
-    rim(wc, 64, 17, 1, 128)
-    for m in range(4):
-        vf[m, 0:128, 0:128] = cf_ref[m]
-        vf[m, 0:128, 128:256] = cs_ref[m]
-        rim(vf.at[m], 128, 2 * m, 2, 256)
-        vc[m, 0:64, :] = cm_ref[m]
-        rim(vc.at[m], 64, 8 + 2 * m, 2, 128)
+    def edges(out, m, size, width, above, below):
+        for row, (both, at) in ((0, (above, 2 * m + 1)), (size - 1, (below, 2 * m))):
+            inner = 1 if row == 0 else size - 2
+            out[m, row:row + 1, :] = out[m, row:row + 1, :] - both[0][at:at + 1, 0:width]
+            out[m, inner:inner + 1, :] = out[m, inner:inner + 1, :] - both[1][at:at + 1, 0:width]
+
+    odd = is_odd("ty")
+    top = jnp.where(odd, with_ref[...], off_ref[...])
+    bottom = jnp.where(odd, off_ref[...], with_ref[...])
+    before = jnp.where(odd, fw_ref[...], fo_ref[...])
+    after = jnp.where(odd, fo_ref[...], fw_ref[...])
+    above = rim(top, before, 0, 16, 256, 1)
+    below = rim(bottom, after, 0, 16, 256, 7)
+    coarse_above = rim(top, before, 8, 17, 128, 1)
+    coarse_below = rim(bottom, after, 8, 17, 128, 7)
     take.wait()
     sends = []
     for m in range(4):
@@ -210,30 +240,31 @@
                 tall[m, spots, :] = part if h == 0 else part + tall[m, spots, :]
         every = [tall[m, pl.ds(8 + k, 64, stride=2), :] for k in range(-2, 3)]
         low[m * 64:(m + 1) * 64, :] = 0.75 * every[2] + 0.5 * (every[1] + every[3]) + 0.125 * (every[0] + every[4])
-        fine_out[m] = lw[0] * tall[m, 8:136, :] - twice(vf[m], wf[...])[0:128, 0:128]
+        fine_out[m] = lw[0] * tall[m, 8:136, :] - bf_ref[m]
+        edges(fine_out, m, 128, 128, above, below)
         send = pltpu.make_async_copy(fine_out.at[m], fine_ref.at[m], sems.at[m])
         send.start()
         sends.append(send)
     coarse = sum(mm(p, halve) for p in split3(low[...]))
     for m in range(4):
-        coarse_out[m] = lw[1] * coarse[m * 64:(m + 1) * 64, 0:64] - twice(vc[m], wc[...])[0:64, 0:64]
+        coarse_out[m] = lw[1] * coarse[m * 64:(m + 1) * 64, 0:64] - bc_ref[m, :, 0:64]
+        edges(coarse_out, m, 64, 64, coarse_above, coarse_below)
     send = pltpu.make_async_copy(coarse_out, coarse_ref, sems.at[4])
     send.start()
     for send in sends + [send]:
         send.wait()
 
 
-def neighbours(axis):
-    count = lax.axis_size(axis)
-    up = [(i, i + 1) for i in range(count - 1)]
-    return up, [(j, i) for i, j in up]
+def swap(x, axis, first):
+    pairs = [(i, i + 1) for i in range(first, lax.axis_size(axis) - 1, 2)]
+    return lax.ppermute(x, axis, pairs + [(j, i) for i, j in pairs])
 
 
 def edges(coef_fine, coef_coarse, kappa_map, kappa_table, at):
     smem = pl.BlockSpec(memory_space=pltpu.SMEM)
     vmem = pl.BlockSpec(memory_space=pltpu.VMEM)
     square = pltpu.VMEM((128, 128), F)
-    to_left, to_right, df, dc = pl.pallas_call(
+    with_x, off_x, df, dc = pl.pallas_call(
         columns_kernel,
         in_specs=[smem] + [vmem] * 3,
         out_shape=[struct(24, 128), struct(24, 128), struct(128, 128), struct(64, 128)],
@@ -241,21 +272,23 @@
         compiler_params=params(),
         name="edge_columns",
     )(kappa_table, coef_fine, coef_coarse, kappa_map)
-    onward, back = neighbours("tx")
-    from_left = lax.ppermute(to_right, "tx", onward)
-    from_right = lax.ppermute(to_left, "tx", back)
-    to_up, to_down, side, coarse, dside, dcoarse = pl.pallas_call(
+    from_with = swap(with_x, "tx", 0)
+    from_off = swap(off_x, "tx", 1)
+    with_y, off_y, fine, coarse = pl.pallas_call(
         rows_kernel,
         in_specs=[vmem] * 6 + [pl.BlockSpec(memory_space=pl.ANY)],
-        out_shape=[struct(24, 256), struct(24, 256), struct(4, 128, 128), struct(4, 64, 128), struct(128, 128), struct(64, 128)],
-        scratch_shapes=[square],
+        out_shape=[struct(24, 256), struct(24, 256), struct(4, 128, 128), struct(4, 64, 128)],
+        scratch_shapes=[
+            square,
+            pltpu.VMEM((4, 136, 256), F),
+            pltpu.VMEM((136, 256), F),
+            pltpu.VMEM((4, 72, 128), F),
+            pltpu.VMEM((72, 128), F),
+        ],
         compiler_params=params(),
         name="edge_rows",
-    )(coef_fine, coef_coarse, df, dc, from_left, from_right, at)
-    onward, back = neighbours("ty")
-    from_up = lax.ppermute(to_down, "ty", onward)
-    from_down = lax.ppermute(to_up, "ty", back)
-    return coef_fine, side, coarse, df, dside, dcoarse, from_up, from_down
+    )(coef_fine, coef_coarse, df, dc, from_with, from_off, at)
+    return fine, coarse, with_y, off_y, swap(with_y, "ty", 0), swap(off_y, "ty", 1)
 
 
 def finish(level_weight, total, fields):
@@ -267,10 +300,6 @@
         out_shape=[struct(4, 128, 128), struct(4, 64, 64)],
         scratch_shapes=[
             pltpu.SMEM((2,), F),
-            pltpu.VMEM((4, 136, 256), F),
-            pltpu.VMEM((136, 256), F),
-            pltpu.VMEM((4, 72, 128), F),
-            pltpu.VMEM((72, 128), F),
             pltpu.VMEM((4, 144, 128), F),
             pltpu.VMEM((256, 128), F),
             pltpu.VMEM((4, 128, 128), F),

time: 59.2 us -> 57.2 us (0.966)
  the two profiles are of different devices: /device:TPU:14 before, /device:TPU:39 now
where the time goes in v4:
time: 57.2 us; the launch traced here: 56.2 us
  Pallas kernels  27 us (47%)
  starting transfers between devices  21.2 us (37%)
  waiting for transfers between devices  6.36 us (11%)
  local copies, waits for them, and re-layouts  0.87 us (2%)
  between operations  0.81 us (1%)
    pallas_call x1, Pallas kernels, project(): pl.pallas_call(functools.partial(project_kernel, group, slots), grid=(til...  15.8 us
    ppermute x4, starting transfers between devices, swap(): return lax.ppermute(x, axis, pairs + [(j, i) for i, j in pairs])  10.7 us
    all_to_all x1, starting transfers between devices, on_device(): lax.all_to_all(packed, AXES, split_axis=0, concat_axis=0, tiled=True)  10.5 us
    ppermute x4, waiting for transfers between devices, swap(): return lax.ppermute(x, axis, pairs + [(j, i) for i, j in pairs])  6.36 us
    pallas_call x1, Pallas kernels, places(): pl.pallas_call(place_kernel, grid=(tiles // group,), in_specs=[points, po...  4.96 us
    pallas_call x1, Pallas kernels, pack(): pl.pallas_call(functools.partial(pack_kernel, block), in_specs=[pl.BlockS...  2.3 us
    pallas_call x1, Pallas kernels, finish(): pl.pallas_call(finish_kernel, in_specs=[pl.BlockSpec(memory_space=pl.ANY)...  1.73 us
    pallas_call x1, Pallas kernels, edges(): pl.pallas_call(rows_kernel, in_specs=[vmem] * 6 + [pl.BlockSpec(memory_sp...  1.42 us
  transfers between devices with their start and end apart: 5, of which 2 were waited for; matrix products, arithmetic and copies ran while one was open for 0% of the time, Pallas kernels for 41%

profile of v4, /device:TPU:39, one launch (start us, length us, event | category | flops | bytes accessed | tf_op | source)
XLA Modules:
  0.0 56.2 jit_solution(14321866313732515499)
XLA Ops:
  0.6 2.3 %pack_rows.1 = f32[3072,128]{1,0:T(8,128)} custom-call(s32[1,128]{1,0:T(1,128)} %counts_ref.1, f32[4,128,768]{2,1,0:T(8,128)} %bitcast.9), custom_call_target="tpu_custom_call" | custom-call | tf_op jit(solution)/shard_map/pack_rows/pallas_call | solution.py:78
  2.9 0.0 copy-start
  3.0 0.0 copy-start.3
  3.0 0.0 copy-start.5
  3.0 0.0 copy-start.1
  3.0 0.0 copy-start.2
  3.0 10.5 %all-to-all-start = ((f32[128,6,4,128]{3,2,1,0:T(4,128)}), f32[128,6,4,128]{3,2,1,0:T(4,128)S(1)}, u32[]{:S(2)}, u32[]{:S(2)}) async-start(f32[128,6,4,128]{3,2,1,0:T(4,128)} %bitcast.8), calls=%async_computation | async-start | bytes 3145728 | tf_op jit(solution)/shard_map/all_to_all | solution.py:418
  13.5 0.0 copy-done
  13.5 0.0 copy-done.3
  13.5 0.0 copy-done.5
  13.5 0.0 copy-start.4
  13.6 0.8 %copy-done.4 = s32[128,128]{1,0:T(8,128)S(1)} copy-done((s32[128,128]{1,0:T(8,128)S(1)}, s32[128,128]{1,0:T(8,128)}, u32[]{:S(2)}) %copy-start.4) | copy-done | bytes 65560
  14.4 0.8 %edge_columns.1 = (f32[24,128]{1,0:T(8,128)S(1)}, f32[24,128]{1,0:T(8,128)S(1)}, f32[128,128]{1,0:T(8,128)S(1)}, f32[64,128]{1,0:T(8,128)S(1)}) custom-call(f32[2,8]{1,0:T(2,128)S(1)} %copy-done.5, f32[4,128,128]{2,1,0:T(8,128)S(1)} %copy-done, f32[4,64,64]{2,1,0:T(8,128)S(1)} %copy-done.3, s32[128,128]{1,0:T(8,128)S(1)} %copy-done.4), custom_call_target="tpu_custom_call" | custom-call | tf_op jit(solution)/shard_map/edge_columns/pallas_call | solution.py:267
  15.2 0.6 %collective-permute-start = (f32[24,128]{1,0:T(8,128)S(1)}, f32[24,128]{1,0:T(8,128)S(1)}, u32[]{:S(2)}, u32[]{:S(2)}) collective-permute-start(f32[24,128]{1,0:T(8,128)S(1)} %get-tuple-element.12), channel_id=1, source_target_pairs={{0,1},{2,3},{4,5},{6,7},{1,0},{3,2},{5,4},{7,6},{8,9},{10,11},{12,... | collective-permute-start | bytes 36872 | tf_op jit(solution)/shard_map/ppermute | solution.py:260
  15.8 4.8 %collective-permute-start.1 = (f32[24,128]{1,0:T(8,128)S(1)}, f32[24,128]{1,0:T(8,128)S(1)}, u32[]{:S(2)}, u32[]{:S(2)}) collective-permute-start(f32[24,128]{1,0:T(8,128)S(1)} %get-tuple-element.13), channel_id=1, source_target_pairs={{1,2},{3,4},{5,6},{2,1},{4,3},{6,5},{9,10},{11,12},{13,14},{10,9},... | collective-permute-start | bytes 36872 | tf_op jit(solution)/shard_map/ppermute | solution.py:260
  20.6 0.0 copy-done.1
  20.6 0.0 copy-done.2
  20.7 5.0 %place_rows.1.at_ref = f32[16,128,768]{2,1,0:T(8,128)} custom-call(s32[2,128,768]{2,1,0:T(8,128)S(1)} %bitcast.6, f32[2,128,768]{2,1,0:T(8,128)S(1)} %bitcast.7), custom_call_target="tpu_custom_call" | custom-call | tf_op jit(solution)/shard_map/place_rows/pallas_call | solution.py:354
  25.6 5.7 %collective-permute-done.fw_ref = f32[24,128]{1,0:T(8,128)S(1)} collective-permute-done((f32[24,128]{1,0:T(8,128)S(1)}, f32[24,128]{1,0:T(8,128)S(1)}, u32[]{:S(2)}, u32[]{:S(2)}) %collective-permute-start) | collective-permute-done | bytes 12320 | tf_op jit(solution)/shard_map/ppermute | solution.py:260
  31.3 0.7 %collective-permute-done.1.fo_ref = f32[24,128]{1,0:T(8,128)S(1)} collective-permute-done((f32[24,128]{1,0:T(8,128)S(1)}, f32[24,128]{1,0:T(8,128)S(1)}, u32[]{:S(2)}, u32[]{:S(2)}) %collective-permute-start.1) | collective-permute-done | bytes 12320 | tf_op jit(solution)/shard_map/ppermute | solution.py:260
  32.0 1.4 %edge_rows.1 = (f32[24,256]{1,0:T(8,128)S(1)}, f32[24,256]{1,0:T(8,128)S(1)}, f32[4,128,128]{2,1,0:T(8,128)S(1)}, f32[4,64,128]{2,1,0:T(8,128)S(1)}) custom-call(f32[4,128,128]{2,1,0:T(8,128)S(1)} %copy-done, f32[4,64,64]{2,1,0:T(8,128)S(1)} %copy-done.3, f32[128,128]{1,0:T(8,128)S(1)} %get-tuple-element.10.df_ref, f32[64,128]{1,0:T(8,128)S(1)} %get-tuple-element.11.dc_ref, ...), custom_call_target="tpu_custom_call" | custom-call | tf_op jit(solution)/shard_map/edge_rows/pallas_call | solution.py:277
  33.4 1.5 %collective-permute-start.2 = (f32[24,256]{1,0:T(8,128)S(1)}, f32[24,256]{1,0:T(8,128)S(1)}, u32[]{:S(2)}, u32[]{:S(2)}) collective-permute-start(f32[24,256]{1,0:T(8,128)S(1)} %get-tuple-element.16.with_ref), channel_id=1, source_target_pairs={{0,8},{16,24},{32,40},{48,56},{64,72},{80,88},{96,104},{112,120},{... | collective-permute-start | bytes 73736 | tf_op jit(solution)/shard_map/ppermute | solution.py:260
  34.8 3.8 %collective-permute-start.3 = (f32[24,256]{1,0:T(8,128)S(1)}, f32[24,256]{1,0:T(8,128)S(1)}, u32[]{:S(2)}, u32[]{:S(2)}) collective-permute-start(f32[24,256]{1,0:T(8,128)S(1)} %get-tuple-element.17.off_ref), channel_id=1, source_target_pairs={{8,16},{24,32},{40,48},{56,64},{72,80},{88,96},{104,112},{16,8},{3... | collective-permute-start | bytes 73736 | tf_op jit(solution)/shard_map/ppermute | solution.py:260
  38.6 0.0 all-to-all-done
  38.6 0.0 copy-start.6
  38.6 15.8 %project_rows.1.acc = f32[256,256]{1,0:T(8,128)S(1)} custom-call(f32[3072,128]{1,0:T(8,128)S(1)} %bitcast.5, f32[16,128,768]{2,1,0:T(8,128)} %place_rows.1.at_ref), custom_call_target="tpu_custom_call" | custom-call | tf_op jit(solution)/shard_map/project_rows/pallas_call | solution.py:400
  54.5 0.0 collective-permute-done.2.fw_ref
  54.5 0.0 collective-permute-done.3.fo_ref
  54.5 0.0 copy-done.6
  54.5 1.7 %finish_tiles.1 = (f32[4,128,128]{2,1,0:T(8,128)}, f32[4,64,64]{2,1,0:T(8,128)}) custom-call(f32[2]{0:T(128)S(1)} %copy-done.6, f32[256,256]{1,0:T(8,128)S(1)} %project_rows.1.acc, f32[4,128,128]{2,1,0:T(8,128)S(1)} %get-tuple-element.14.bf_ref, f32[4,64,128]{2,1,0:T(8,128)S(1)} %get-tuple-element.15.bc_ref, f32[24,256]{1,0:T(8,128)S(1)} %get-tuple-element.16.with_ref, ...), custom_call_target="tpu_custom_call" | custom-call | tf_op jit(solution)/shard_map/finish_tiles/pallas_call | solution.py:296
Async XLA Ops:
  2.9 10.6 %copy-start = (f32[4,128,128]{2,1,0:T(8,128)S(1)}, f32[4,128,128]{2,1,0:T(8,128)}, u32[]{:S(2)}) copy-start(f32[4,128,128]{2,1,0:T(8,128)} %cf_ref.3) | copy-start | bytes 786436
  3.0 10.6 %copy-start.3 = (f32[4,64,64]{2,1,0:T(8,128)S(1)}, f32[4,64,64]{2,1,0:T(8,128)}, u32[]{:S(2)}) copy-start(f32[4,64,64]{2,1,0:T(8,128)} %cc_ref.3) | copy-start | bytes 196612
  3.0 10.6 %copy-start.5 = (f32[2,8]{1,0:T(2,128)S(1)}, f32[2,8]{1,0:T(2,128)}, u32[]{:S(2)}) copy-start(f32[2,8]{1,0:T(2,128)} %table_ref.1) | copy-start | bytes 196
  3.0 17.7 %copy-start.1 = (s32[1,2,128,768]{3,2,1,0:T(8,128)S(1)}, s32[1,2,128,768]{3,2,1,0:T(8,128)}, u32[]{:S(2)}) copy-start(s32[1,2,128,768]{3,2,1,0:T(8,128)} %param.11) | copy-start | bytes 2359300
  3.0 17.7 %copy-start.2 = (f32[1,2,128,768]{3,2,1,0:T(8,128)S(1)}, f32[1,2,128,768]{3,2,1,0:T(8,128)}, u32[]{:S(2)}) copy-start(f32[1,2,128,768]{3,2,1,0:T(8,128)} %param.12) | copy-start | bytes 2359300
  3.0 35.6 %all-to-all-start = ((f32[128,6,4,128]{3,2,1,0:T(4,128)}), f32[128,6,4,128]{3,2,1,0:T(4,128)S(1)}, u32[]{:S(2)}, u32[]{:S(2)}) async-start(f32[128,6,4,128]{3,2,1,0:T(4,128)} %bitcast.8), calls=%async_computation | async-start | bytes 3145728 | tf_op jit(solution)/shard_map/all_to_all | solution.py:418
  13.5 0.8 %copy-start.4 = (s32[128,128]{1,0:T(8,128)S(1)}, s32[128,128]{1,0:T(8,128)}, u32[]{:S(2)}) copy-start(s32[128,128]{1,0:T(8,128)} %km_ref.1) | copy-start | bytes 196612
  15.2 16.1 %collective-permute-start = (f32[24,128]{1,0:T(8,128)S(1)}, f32[24,128]{1,0:T(8,128)S(1)}, u32[]{:S(2)}, u32[]{:S(2)}) collective-permute-start(f32[24,128]{1,0:T(8,128)S(1)} %get-tuple-element.12), channel_id=1, source_target_pairs={{0,1},{2,3},{4,5},{6,7},{1,0},{3,2},{5,4},{7,6},{8,9},{10,11},{12,... | collective-permute-start | bytes 36872 | tf_op jit(solution)/shard_map/ppermute | solution.py:260
  15.8 16.2 %collective-permute-start.1 = (f32[24,128]{1,0:T(8,128)S(1)}, f32[24,128]{1,0:T(8,128)S(1)}, u32[]{:S(2)}, u32[]{:S(2)}) collective-permute-start(f32[24,128]{1,0:T(8,128)S(1)} %get-tuple-element.13), channel_id=1, source_target_pairs={{1,2},{3,4},{5,6},{2,1},{4,3},{6,5},{9,10},{11,12},{13,14},{10,9},... | collective-permute-start | bytes 36872 | tf_op jit(solution)/shard_map/ppermute | solution.py:260
  33.4 21.1 %collective-permute-start.2 = (f32[24,256]{1,0:T(8,128)S(1)}, f32[24,256]{1,0:T(8,128)S(1)}, u32[]{:S(2)}, u32[]{:S(2)}) collective-permute-start(f32[24,256]{1,0:T(8,128)S(1)} %get-tuple-element.16.with_ref), channel_id=1, source_target_pairs={{0,8},{16,24},{32,40},{48,56},{64,72},{80,88},{96,104},{112,120},{... | collective-permute-start | bytes 73736 | tf_op jit(solution)/shard_map/ppermute | solution.py:260
  34.8 19.6 %collective-permute-start.3 = (f32[24,256]{1,0:T(8,128)S(1)}, f32[24,256]{1,0:T(8,128)S(1)}, u32[]{:S(2)}, u32[]{:S(2)}) collective-permute-start(f32[24,256]{1,0:T(8,128)S(1)} %get-tuple-element.17.off_ref), channel_id=1, source_target_pairs={{8,16},{24,32},{40,48},{56,64},{72,80},{88,96},{104,112},{16,8},{3... | collective-permute-start | bytes 73736 | tf_op jit(solution)/shard_map/ppermute | solution.py:260
  38.6 15.8 %copy-start.6 = (f32[2]{0:T(128)S(1)}, f32[2]{0:T(128)}, u32[]{:S(2)}) copy-start(f32[2]{0:T(128)} %lw_ref.1) | copy-start | bytes 28

commit v5 on v4

--- a/solution.py
+++ b/solution.py
@@ -368,10 +368,16 @@
         acc[...] = jnp.zeros_like(acc)
 
     chunks = slots // 128
-    for m in range(4):
-        v = jnp.concatenate([v_ref[pl.ds(4 * kc + m, group, stride=4 * chunks), :] for kc in range(chunks)], 1)
+    base = pl.multiple_of(pl.program_id(0) * (group * 4 * chunks), group * 4 * chunks)
+
+    def weigh(first, m):
+        rows = [v_ref[pl.ds(base + (first * chunks + kc) * 4 + m, 8, stride=4 * chunks), :] for kc in range(chunks)]
+        v = jnp.concatenate(rows, 1)
         for r in range(4):
-            values[4 * m + r] = v * at_ref[12 + r]
+            values[4 * m + r, first:first + 8, :] = v * at_ref[12 + r, first:first + 8, :]
+
+    for m in range(4):
+        weigh(0, m)
     i16 = iota((16, slots), 0).astype(F).astype(BF)
     i64 = iota((64, slots), 0).astype(F).astype(BF)
     zero = jnp.zeros((), BF)
@@ -390,6 +396,8 @@
         return jnp.concatenate(left, 0), jnp.concatenate(right, 0)
 
     for s in range(group):
+        if s + 8 < group and s % 2 == 1:
+            weigh(s // 8 * 8 + 8, s % 8 // 2)
         left, right = build(s)
         acc[...] += mm(left, right, ((1,), (1,)))
 
@@ -401,7 +409,7 @@
         functools.partial(project_kernel, group, slots),
         grid=(tiles // group,),
         in_specs=[
-            pl.BlockSpec((group * slots // 32, 128), lambda i: (i, 0)),
+            pl.BlockSpec(memory_space=pltpu.VMEM),
             pl.BlockSpec((16, group, slots), lambda i: (0, i, 0)),
         ],
         out_specs=pl.BlockSpec((256, 256), lambda i: (0, 0)),

time: 57.2 us -> 57.2 us (level)
  no operation moved by 1% of the time
where the time goes in v5:
time: 57.2 us; the launch traced here: 56.2 us
  Pallas kernels  27 us (47%)
  starting transfers between devices  21.2 us (37%)
  waiting for transfers between devices  6.36 us (11%)
  local copies, waits for them, and re-layouts  0.87 us (2%)
  between operations  0.81 us (1%)
    pallas_call x1, Pallas kernels, project(): pl.pallas_call(functools.partial(project_kernel, group, slots), grid=(til...  15.8 us
    ppermute x4, starting transfers between devices, swap(): return lax.ppermute(x, axis, pairs + [(j, i) for i, j in pairs])  10.7 us
    all_to_all x1, starting transfers between devices, on_device(): lax.all_to_all(packed, AXES, split_axis=0, concat_axis=0, tiled=True)  10.5 us
    ppermute x4, waiting for transfers between devices, swap(): return lax.ppermute(x, axis, pairs + [(j, i) for i, j in pairs])  6.36 us
    pallas_call x1, Pallas kernels, places(): pl.pallas_call(place_kernel, grid=(tiles // group,), in_specs=[points, po...  4.96 us
    pallas_call x1, Pallas kernels, pack(): pl.pallas_call(functools.partial(pack_kernel, block), in_specs=[pl.BlockS...  2.3 us
    pallas_call x1, Pallas kernels, finish(): pl.pallas_call(finish_kernel, in_specs=[pl.BlockSpec(memory_space=pl.ANY)...  1.73 us
    pallas_call x1, Pallas kernels, edges(): pl.pallas_call(rows_kernel, in_specs=[vmem] * 6 + [pl.BlockSpec(memory_sp...  1.42 us
  transfers between devices with their start and end apart: 5, of which 2 were waited for; matrix products, arithmetic and copies ran while one was open for 0% of the time, Pallas kernels for 41%

profile of v5, /device:TPU:39, one launch (start us, length us, event | category | flops | bytes accessed | tf_op | source)
XLA Modules:
  0.0 56.2 jit_solution(15898224469486847872)
XLA Ops:
  0.6 2.3 %pack_rows.1 = f32[3072,128]{1,0:T(8,128)} custom-call(s32[1,128]{1,0:T(1,128)} %counts_ref.1, f32[4,128,768]{2,1,0:T(8,128)} %bitcast.9), custom_call_target="tpu_custom_call" | custom-call | tf_op jit(solution)/shard_map/pack_rows/pallas_call | solution.py:78
  2.9 0.0 copy-start
  3.0 0.0 copy-start.3
  3.0 0.0 copy-start.5
  3.0 0.0 copy-start.1
  3.0 0.0 copy-start.2
  3.0 10.5 %all-to-all-start = ((f32[128,6,4,128]{3,2,1,0:T(4,128)}), f32[128,6,4,128]{3,2,1,0:T(4,128)S(1)}, u32[]{:S(2)}, u32[]{:S(2)}) async-start(f32[128,6,4,128]{3,2,1,0:T(4,128)} %bitcast.8), calls=%async_computation | async-start | bytes 3145728 | tf_op jit(solution)/shard_map/all_to_all | solution.py:426
  13.5 0.0 copy-done
  13.5 0.0 copy-done.3
  13.5 0.0 copy-done.5
  13.5 0.0 copy-start.4
  13.6 0.8 %copy-done.4 = s32[128,128]{1,0:T(8,128)S(1)} copy-done((s32[128,128]{1,0:T(8,128)S(1)}, s32[128,128]{1,0:T(8,128)}, u32[]{:S(2)}) %copy-start.4) | copy-done | bytes 65560
  14.4 0.8 %edge_columns.1 = (f32[24,128]{1,0:T(8,128)S(1)}, f32[24,128]{1,0:T(8,128)S(1)}, f32[128,128]{1,0:T(8,128)S(1)}, f32[64,128]{1,0:T(8,128)S(1)}) custom-call(f32[2,8]{1,0:T(2,128)S(1)} %copy-done.5, f32[4,128,128]{2,1,0:T(8,128)S(1)} %copy-done, f32[4,64,64]{2,1,0:T(8,128)S(1)} %copy-done.3, s32[128,128]{1,0:T(8,128)S(1)} %copy-done.4), custom_call_target="tpu_custom_call" | custom-call | tf_op jit(solution)/shard_map/edge_columns/pallas_call | solution.py:267
  15.2 0.6 %collective-permute-start = (f32[24,128]{1,0:T(8,128)S(1)}, f32[24,128]{1,0:T(8,128)S(1)}, u32[]{:S(2)}, u32[]{:S(2)}) collective-permute-start(f32[24,128]{1,0:T(8,128)S(1)} %get-tuple-element.12), channel_id=1, source_target_pairs={{0,1},{2,3},{4,5},{6,7},{1,0},{3,2},{5,4},{7,6},{8,9},{10,11},{12,... | collective-permute-start | bytes 36872 | tf_op jit(solution)/shard_map/ppermute | solution.py:260
  15.8 4.8 %collective-permute-start.1 = (f32[24,128]{1,0:T(8,128)S(1)}, f32[24,128]{1,0:T(8,128)S(1)}, u32[]{:S(2)}, u32[]{:S(2)}) collective-permute-start(f32[24,128]{1,0:T(8,128)S(1)} %get-tuple-element.13), channel_id=1, source_target_pairs={{1,2},{3,4},{5,6},{2,1},{4,3},{6,5},{9,10},{11,12},{13,14},{10,9},... | collective-permute-start | bytes 36872 | tf_op jit(solution)/shard_map/ppermute | solution.py:260
  20.6 0.0 copy-done.1
  20.6 0.0 copy-done.2
  20.7 5.0 %place_rows.1.at_ref = f32[16,128,768]{2,1,0:T(8,128)} custom-call(s32[2,128,768]{2,1,0:T(8,128)S(1)} %bitcast.6, f32[2,128,768]{2,1,0:T(8,128)S(1)} %bitcast.7), custom_call_target="tpu_custom_call" | custom-call | tf_op jit(solution)/shard_map/place_rows/pallas_call | solution.py:354
  25.6 5.7 %collective-permute-done.fw_ref = f32[24,128]{1,0:T(8,128)S(1)} collective-permute-done((f32[24,128]{1,0:T(8,128)S(1)}, f32[24,128]{1,0:T(8,128)S(1)}, u32[]{:S(2)}, u32[]{:S(2)}) %collective-permute-start) | collective-permute-done | bytes 12320 | tf_op jit(solution)/shard_map/ppermute | solution.py:260
  31.3 0.7 %collective-permute-done.1.fo_ref = f32[24,128]{1,0:T(8,128)S(1)} collective-permute-done((f32[24,128]{1,0:T(8,128)S(1)}, f32[24,128]{1,0:T(8,128)S(1)}, u32[]{:S(2)}, u32[]{:S(2)}) %collective-permute-start.1) | collective-permute-done | bytes 12320 | tf_op jit(solution)/shard_map/ppermute | solution.py:260
  32.0 1.4 %edge_rows.1 = (f32[24,256]{1,0:T(8,128)S(1)}, f32[24,256]{1,0:T(8,128)S(1)}, f32[4,128,128]{2,1,0:T(8,128)S(1)}, f32[4,64,128]{2,1,0:T(8,128)S(1)}) custom-call(f32[4,128,128]{2,1,0:T(8,128)S(1)} %copy-done, f32[4,64,64]{2,1,0:T(8,128)S(1)} %copy-done.3, f32[128,128]{1,0:T(8,128)S(1)} %get-tuple-element.10.df_ref, f32[64,128]{1,0:T(8,128)S(1)} %get-tuple-element.11.dc_ref, ...), custom_call_target="tpu_custom_call" | custom-call | tf_op jit(solution)/shard_map/edge_rows/pallas_call | solution.py:277
  33.4 1.5 %collective-permute-start.2 = (f32[24,256]{1,0:T(8,128)S(1)}, f32[24,256]{1,0:T(8,128)S(1)}, u32[]{:S(2)}, u32[]{:S(2)}) collective-permute-start(f32[24,256]{1,0:T(8,128)S(1)} %get-tuple-element.16.with_ref), channel_id=1, source_target_pairs={{0,8},{16,24},{32,40},{48,56},{64,72},{80,88},{96,104},{112,120},{... | collective-permute-start | bytes 73736 | tf_op jit(solution)/shard_map/ppermute | solution.py:260
  34.8 3.8 %collective-permute-start.3 = (f32[24,256]{1,0:T(8,128)S(1)}, f32[24,256]{1,0:T(8,128)S(1)}, u32[]{:S(2)}, u32[]{:S(2)}) collective-permute-start(f32[24,256]{1,0:T(8,128)S(1)} %get-tuple-element.17.off_ref), channel_id=1, source_target_pairs={{8,16},{24,32},{40,48},{56,64},{72,80},{88,96},{104,112},{16,8},{3... | collective-permute-start | bytes 73736 | tf_op jit(solution)/shard_map/ppermute | solution.py:260
  38.6 0.0 all-to-all-done
  38.6 0.0 copy-start.6
  38.6 15.8 %project_rows.1.acc = f32[256,256]{1,0:T(8,128)S(1)} custom-call(f32[3072,128]{1,0:T(8,128)S(1)} %bitcast.5, f32[16,128,768]{2,1,0:T(8,128)} %place_rows.1.at_ref), custom_call_target="tpu_custom_call" | custom-call | tf_op jit(solution)/shard_map/project_rows/pallas_call | solution.py:408
  54.5 0.0 collective-permute-done.2.fw_ref
  54.5 0.0 collective-permute-done.3.fo_ref
  54.5 0.0 copy-done.6
  54.5 1.7 %finish_tiles.1 = (f32[4,128,128]{2,1,0:T(8,128)}, f32[4,64,64]{2,1,0:T(8,128)}) custom-call(f32[2]{0:T(128)S(1)} %copy-done.6, f32[256,256]{1,0:T(8,128)S(1)} %project_rows.1.acc, f32[4,128,128]{2,1,0:T(8,128)S(1)} %get-tuple-element.14.bf_ref, f32[4,64,128]{2,1,0:T(8,128)S(1)} %get-tuple-element.15.bc_ref, f32[24,256]{1,0:T(8,128)S(1)} %get-tuple-element.16.with_ref, ...), custom_call_target="tpu_custom_call" | custom-call | tf_op jit(solution)/shard_map/finish_tiles/pallas_call | solution.py:296
Async XLA Ops:
  2.9 10.6 %copy-start = (f32[4,128,128]{2,1,0:T(8,128)S(1)}, f32[4,128,128]{2,1,0:T(8,128)}, u32[]{:S(2)}) copy-start(f32[4,128,128]{2,1,0:T(8,128)} %cf_ref.3) | copy-start | bytes 786436
  3.0 10.6 %copy-start.3 = (f32[4,64,64]{2,1,0:T(8,128)S(1)}, f32[4,64,64]{2,1,0:T(8,128)}, u32[]{:S(2)}) copy-start(f32[4,64,64]{2,1,0:T(8,128)} %cc_ref.3) | copy-start | bytes 196612
  3.0 10.6 %copy-start.5 = (f32[2,8]{1,0:T(2,128)S(1)}, f32[2,8]{1,0:T(2,128)}, u32[]{:S(2)}) copy-start(f32[2,8]{1,0:T(2,128)} %table_ref.1) | copy-start | bytes 196
  3.0 17.7 %copy-start.1 = (s32[1,2,128,768]{3,2,1,0:T(8,128)S(1)}, s32[1,2,128,768]{3,2,1,0:T(8,128)}, u32[]{:S(2)}) copy-start(s32[1,2,128,768]{3,2,1,0:T(8,128)} %param.11) | copy-start | bytes 2359300
  3.0 17.7 %copy-start.2 = (f32[1,2,128,768]{3,2,1,0:T(8,128)S(1)}, f32[1,2,128,768]{3,2,1,0:T(8,128)}, u32[]{:S(2)}) copy-start(f32[1,2,128,768]{3,2,1,0:T(8,128)} %param.12) | copy-start | bytes 2359300
  3.0 35.6 %all-to-all-start = ((f32[128,6,4,128]{3,2,1,0:T(4,128)}), f32[128,6,4,128]{3,2,1,0:T(4,128)S(1)}, u32[]{:S(2)}, u32[]{:S(2)}) async-start(f32[128,6,4,128]{3,2,1,0:T(4,128)} %bitcast.8), calls=%async_computation | async-start | bytes 3145728 | tf_op jit(solution)/shard_map/all_to_all | solution.py:426
  13.5 0.8 %copy-start.4 = (s32[128,128]{1,0:T(8,128)S(1)}, s32[128,128]{1,0:T(8,128)}, u32[]{:S(2)}) copy-start(s32[128,128]{1,0:T(8,128)} %km_ref.1) | copy-start | bytes 196612
  15.2 16.1 %collective-permute-start = (f32[24,128]{1,0:T(8,128)S(1)}, f32[24,128]{1,0:T(8,128)S(1)}, u32[]{:S(2)}, u32[]{:S(2)}) collective-permute-start(f32[24,128]{1,0:T(8,128)S(1)} %get-tuple-element.12), channel_id=1, source_target_pairs={{0,1},{2,3},{4,5},{6,7},{1,0},{3,2},{5,4},{7,6},{8,9},{10,11},{12,... | collective-permute-start | bytes 36872 | tf_op jit(solution)/shard_map/ppermute | solution.py:260
  15.8 16.2 %collective-permute-start.1 = (f32[24,128]{1,0:T(8,128)S(1)}, f32[24,128]{1,0:T(8,128)S(1)}, u32[]{:S(2)}, u32[]{:S(2)}) collective-permute-start(f32[24,128]{1,0:T(8,128)S(1)} %get-tuple-element.13), channel_id=1, source_target_pairs={{1,2},{3,4},{5,6},{2,1},{4,3},{6,5},{9,10},{11,12},{13,14},{10,9},... | collective-permute-start | bytes 36872 | tf_op jit(solution)/shard_map/ppermute | solution.py:260
  33.4 21.1 %collective-permute-start.2 = (f32[24,256]{1,0:T(8,128)S(1)}, f32[24,256]{1,0:T(8,128)S(1)}, u32[]{:S(2)}, u32[]{:S(2)}) collective-permute-start(f32[24,256]{1,0:T(8,128)S(1)} %get-tuple-element.16.with_ref), channel_id=1, source_target_pairs={{0,8},{16,24},{32,40},{48,56},{64,72},{80,88},{96,104},{112,120},{... | collective-permute-start | bytes 73736 | tf_op jit(solution)/shard_map/ppermute | solution.py:260
  34.8 19.6 %collective-permute-start.3 = (f32[24,256]{1,0:T(8,128)S(1)}, f32[24,256]{1,0:T(8,128)S(1)}, u32[]{:S(2)}, u32[]{:S(2)}) collective-permute-start(f32[24,256]{1,0:T(8,128)S(1)} %get-tuple-element.17.off_ref), channel_id=1, source_target_pairs={{8,16},{24,32},{40,48},{56,64},{72,80},{88,96},{104,112},{16,8},{3... | collective-permute-start | bytes 73736 | tf_op jit(solution)/shard_map/ppermute | solution.py:260
  38.6 15.8 %copy-start.6 = (f32[2]{0:T(128)S(1)}, f32[2]{0:T(128)}, u32[]{:S(2)}) copy-start(f32[2]{0:T(128)} %lw_ref.1) | copy-start | bytes 28

commit v6 on v5

--- a/solution.py
+++ b/solution.py
@@ -395,11 +395,15 @@
         right = [jnp.where(i64 == spread(at_ref, 4 + r, s, 64), spread(at_ref, 8 + r, s, 64), zero) for r in range(4)]
         return jnp.concatenate(left, 0), jnp.concatenate(right, 0)
 
+    held = []
     for s in range(group):
         if s + 8 < group and s % 2 == 1:
             weigh(s // 8 * 8 + 8, s % 8 // 2)
-        left, right = build(s)
-        acc[...] += mm(left, right, ((1,), (1,)))
+        held.append(build(s))
+        if len(held) == 4:
+            left, right = (jnp.concatenate(side, 1) for side in zip(*held))
+            acc[...] += mm(left, right, ((1,), (1,)))
+            held.clear()
 
 
 def project(values, at):

time: 57.2 us -> 57.2 us (level)
  no operation moved by 1% of the time
where the time goes in v6:
time: 57.2 us; the launch traced here: 56.2 us
  Pallas kernels  27 us (47%)
  starting transfers between devices  21.2 us (37%)
  waiting for transfers between devices  6.36 us (11%)
  local copies, waits for them, and re-layouts  0.87 us (2%)
  between operations  0.81 us (1%)
    pallas_call x1, Pallas kernels, project(): pl.pallas_call(functools.partial(project_kernel, group, slots), grid=(til...  15.8 us
    ppermute x4, starting transfers between devices, swap(): return lax.ppermute(x, axis, pairs + [(j, i) for i, j in pairs])  10.7 us
    all_to_all x1, starting transfers between devices, on_device(): lax.all_to_all(packed, AXES, split_axis=0, concat_axis=0, tiled=True)  10.5 us
    ppermute x4, waiting for transfers between devices, swap(): return lax.ppermute(x, axis, pairs + [(j, i) for i, j in pairs])  6.36 us
    pallas_call x1, Pallas kernels, places(): pl.pallas_call(place_kernel, grid=(tiles // group,), in_specs=[points, po...  4.96 us
    pallas_call x1, Pallas kernels, pack(): pl.pallas_call(functools.partial(pack_kernel, block), in_specs=[pl.BlockS...  2.3 us
    pallas_call x1, Pallas kernels, finish(): pl.pallas_call(finish_kernel, in_specs=[pl.BlockSpec(memory_space=pl.ANY)...  1.73 us
    pallas_call x1, Pallas kernels, edges(): pl.pallas_call(rows_kernel, in_specs=[vmem] * 6 + [pl.BlockSpec(memory_sp...  1.42 us
  transfers between devices with their start and end apart: 5, of which 2 were waited for; matrix products, arithmetic and copies ran while one was open for 0% of the time, Pallas kernels for 41%

profile of v6, /device:TPU:39, one launch (start us, length us, event | category | flops | bytes accessed | tf_op | source)
XLA Modules:
  0.0 56.2 jit_solution(15898224469486847872)
XLA Ops:
  0.6 2.3 %pack_rows.1 = f32[3072,128]{1,0:T(8,128)} custom-call(s32[1,128]{1,0:T(1,128)} %counts_ref.1, f32[4,128,768]{2,1,0:T(8,128)} %bitcast.9), custom_call_target="tpu_custom_call" | custom-call | tf_op jit(solution)/shard_map/pack_rows/pallas_call | solution.py:78
  2.9 0.0 copy-start
  3.0 0.0 copy-start.3
  3.0 0.0 copy-start.5
  3.0 0.0 copy-start.1
  3.0 0.0 copy-start.2
  3.0 10.5 %all-to-all-start = ((f32[128,6,4,128]{3,2,1,0:T(4,128)}), f32[128,6,4,128]{3,2,1,0:T(4,128)S(1)}, u32[]{:S(2)}, u32[]{:S(2)}) async-start(f32[128,6,4,128]{3,2,1,0:T(4,128)} %bitcast.8), calls=%async_computation | async-start | bytes 3145728 | tf_op jit(solution)/shard_map/all_to_all | solution.py:430
  13.5 0.0 copy-done
  13.5 0.0 copy-done.3
  13.5 0.0 copy-done.5
  13.5 0.0 copy-start.4
  13.6 0.8 %copy-done.4 = s32[128,128]{1,0:T(8,128)S(1)} copy-done((s32[128,128]{1,0:T(8,128)S(1)}, s32[128,128]{1,0:T(8,128)}, u32[]{:S(2)}) %copy-start.4) | copy-done | bytes 65560
  14.4 0.8 %edge_columns.1 = (f32[24,128]{1,0:T(8,128)S(1)}, f32[24,128]{1,0:T(8,128)S(1)}, f32[128,128]{1,0:T(8,128)S(1)}, f32[64,128]{1,0:T(8,128)S(1)}) custom-call(f32[2,8]{1,0:T(2,128)S(1)} %copy-done.5, f32[4,128,128]{2,1,0:T(8,128)S(1)} %copy-done, f32[4,64,64]{2,1,0:T(8,128)S(1)} %copy-done.3, s32[128,128]{1,0:T(8,128)S(1)} %copy-done.4), custom_call_target="tpu_custom_call" | custom-call | tf_op jit(solution)/shard_map/edge_columns/pallas_call | solution.py:267
  15.2 0.6 %collective-permute-start = (f32[24,128]{1,0:T(8,128)S(1)}, f32[24,128]{1,0:T(8,128)S(1)}, u32[]{:S(2)}, u32[]{:S(2)}) collective-permute-start(f32[24,128]{1,0:T(8,128)S(1)} %get-tuple-element.12), channel_id=1, source_target_pairs={{0,1},{2,3},{4,5},{6,7},{1,0},{3,2},{5,4},{7,6},{8,9},{10,11},{12,... | collective-permute-start | bytes 36872 | tf_op jit(solution)/shard_map/ppermute | solution.py:260
  15.8 4.8 %collective-permute-start.1 = (f32[24,128]{1,0:T(8,128)S(1)}, f32[24,128]{1,0:T(8,128)S(1)}, u32[]{:S(2)}, u32[]{:S(2)}) collective-permute-start(f32[24,128]{1,0:T(8,128)S(1)} %get-tuple-element.13), channel_id=1, source_target_pairs={{1,2},{3,4},{5,6},{2,1},{4,3},{6,5},{9,10},{11,12},{13,14},{10,9},... | collective-permute-start | bytes 36872 | tf_op jit(solution)/shard_map/ppermute | solution.py:260
  20.6 0.0 copy-done.1
  20.6 0.0 copy-done.2
  20.7 5.0 %place_rows.1.at_ref = f32[16,128,768]{2,1,0:T(8,128)} custom-call(s32[2,128,768]{2,1,0:T(8,128)S(1)} %bitcast.6, f32[2,128,768]{2,1,0:T(8,128)S(1)} %bitcast.7), custom_call_target="tpu_custom_call" | custom-call | tf_op jit(solution)/shard_map/place_rows/pallas_call | solution.py:354
  25.6 5.7 %collective-permute-done.fw_ref = f32[24,128]{1,0:T(8,128)S(1)} collective-permute-done((f32[24,128]{1,0:T(8,128)S(1)}, f32[24,128]{1,0:T(8,128)S(1)}, u32[]{:S(2)}, u32[]{:S(2)}) %collective-permute-start) | collective-permute-done | bytes 12320 | tf_op jit(solution)/shard_map/ppermute | solution.py:260
  31.3 0.7 %collective-permute-done.1.fo_ref = f32[24,128]{1,0:T(8,128)S(1)} collective-permute-done((f32[24,128]{1,0:T(8,128)S(1)}, f32[24,128]{1,0:T(8,128)S(1)}, u32[]{:S(2)}, u32[]{:S(2)}) %collective-permute-start.1) | collective-permute-done | bytes 12320 | tf_op jit(solution)/shard_map/ppermute | solution.py:260
  32.0 1.4 %edge_rows.1 = (f32[24,256]{1,0:T(8,128)S(1)}, f32[24,256]{1,0:T(8,128)S(1)}, f32[4,128,128]{2,1,0:T(8,128)S(1)}, f32[4,64,128]{2,1,0:T(8,128)S(1)}) custom-call(f32[4,128,128]{2,1,0:T(8,128)S(1)} %copy-done, f32[4,64,64]{2,1,0:T(8,128)S(1)} %copy-done.3, f32[128,128]{1,0:T(8,128)S(1)} %get-tuple-element.10.df_ref, f32[64,128]{1,0:T(8,128)S(1)} %get-tuple-element.11.dc_ref, ...), custom_call_target="tpu_custom_call" | custom-call | tf_op jit(solution)/shard_map/edge_rows/pallas_call | solution.py:277
  33.4 1.5 %collective-permute-start.2 = (f32[24,256]{1,0:T(8,128)S(1)}, f32[24,256]{1,0:T(8,128)S(1)}, u32[]{:S(2)}, u32[]{:S(2)}) collective-permute-start(f32[24,256]{1,0:T(8,128)S(1)} %get-tuple-element.16.with_ref), channel_id=1, source_target_pairs={{0,8},{16,24},{32,40},{48,56},{64,72},{80,88},{96,104},{112,120},{... | collective-permute-start | bytes 73736 | tf_op jit(solution)/shard_map/ppermute | solution.py:260
  34.8 3.8 %collective-permute-start.3 = (f32[24,256]{1,0:T(8,128)S(1)}, f32[24,256]{1,0:T(8,128)S(1)}, u32[]{:S(2)}, u32[]{:S(2)}) collective-permute-start(f32[24,256]{1,0:T(8,128)S(1)} %get-tuple-element.17.off_ref), channel_id=1, source_target_pairs={{8,16},{24,32},{40,48},{56,64},{72,80},{88,96},{104,112},{16,8},{3... | collective-permute-start | bytes 73736 | tf_op jit(solution)/shard_map/ppermute | solution.py:260
  38.6 0.0 all-to-all-done
  38.6 0.0 copy-start.6
  38.6 15.8 %project_rows.1.acc = f32[256,256]{1,0:T(8,128)S(1)} custom-call(f32[3072,128]{1,0:T(8,128)S(1)} %bitcast.5, f32[16,128,768]{2,1,0:T(8,128)} %place_rows.1.at_ref), custom_call_target="tpu_custom_call" | custom-call | tf_op jit(solution)/shard_map/project_rows/pallas_call | solution.py:412
  54.5 0.0 collective-permute-done.2.fw_ref
  54.5 0.0 collective-permute-done.3.fo_ref
  54.5 0.0 copy-done.6
  54.5 1.7 %finish_tiles.1 = (f32[4,128,128]{2,1,0:T(8,128)}, f32[4,64,64]{2,1,0:T(8,128)}) custom-call(f32[2]{0:T(128)S(1)} %copy-done.6, f32[256,256]{1,0:T(8,128)S(1)} %project_rows.1.acc, f32[4,128,128]{2,1,0:T(8,128)S(1)} %get-tuple-element.14.bf_ref, f32[4,64,128]{2,1,0:T(8,128)S(1)} %get-tuple-element.15.bc_ref, f32[24,256]{1,0:T(8,128)S(1)} %get-tuple-element.16.with_ref, ...), custom_call_target="tpu_custom_call" | custom-call | tf_op jit(solution)/shard_map/finish_tiles/pallas_call | solution.py:296
Async XLA Ops:
  2.9 10.6 %copy-start = (f32[4,128,128]{2,1,0:T(8,128)S(1)}, f32[4,128,128]{2,1,0:T(8,128)}, u32[]{:S(2)}) copy-start(f32[4,128,128]{2,1,0:T(8,128)} %cf_ref.3) | copy-start | bytes 786436
  3.0 10.6 %copy-start.3 = (f32[4,64,64]{2,1,0:T(8,128)S(1)}, f32[4,64,64]{2,1,0:T(8,128)}, u32[]{:S(2)}) copy-start(f32[4,64,64]{2,1,0:T(8,128)} %cc_ref.3) | copy-start | bytes 196612
  3.0 10.6 %copy-start.5 = (f32[2,8]{1,0:T(2,128)S(1)}, f32[2,8]{1,0:T(2,128)}, u32[]{:S(2)}) copy-start(f32[2,8]{1,0:T(2,128)} %table_ref.1) | copy-start | bytes 196
  3.0 17.7 %copy-start.1 = (s32[1,2,128,768]{3,2,1,0:T(8,128)S(1)}, s32[1,2,128,768]{3,2,1,0:T(8,128)}, u32[]{:S(2)}) copy-start(s32[1,2,128,768]{3,2,1,0:T(8,128)} %param.11) | copy-start | bytes 2359300
  3.0 17.7 %copy-start.2 = (f32[1,2,128,768]{3,2,1,0:T(8,128)S(1)}, f32[1,2,128,768]{3,2,1,0:T(8,128)}, u32[]{:S(2)}) copy-start(f32[1,2,128,768]{3,2,1,0:T(8,128)} %param.12) | copy-start | bytes 2359300
  3.0 35.6 %all-to-all-start = ((f32[128,6,4,128]{3,2,1,0:T(4,128)}), f32[128,6,4,128]{3,2,1,0:T(4,128)S(1)}, u32[]{:S(2)}, u32[]{:S(2)}) async-start(f32[128,6,4,128]{3,2,1,0:T(4,128)} %bitcast.8), calls=%async_computation | async-start | bytes 3145728 | tf_op jit(solution)/shard_map/all_to_all | solution.py:430
  13.5 0.8 %copy-start.4 = (s32[128,128]{1,0:T(8,128)S(1)}, s32[128,128]{1,0:T(8,128)}, u32[]{:S(2)}) copy-start(s32[128,128]{1,0:T(8,128)} %km_ref.1) | copy-start | bytes 196612
  15.2 16.1 %collective-permute-start = (f32[24,128]{1,0:T(8,128)S(1)}, f32[24,128]{1,0:T(8,128)S(1)}, u32[]{:S(2)}, u32[]{:S(2)}) collective-permute-start(f32[24,128]{1,0:T(8,128)S(1)} %get-tuple-element.12), channel_id=1, source_target_pairs={{0,1},{2,3},{4,5},{6,7},{1,0},{3,2},{5,4},{7,6},{8,9},{10,11},{12,... | collective-permute-start | bytes 36872 | tf_op jit(solution)/shard_map/ppermute | solution.py:260
  15.8 16.2 %collective-permute-start.1 = (f32[24,128]{1,0:T(8,128)S(1)}, f32[24,128]{1,0:T(8,128)S(1)}, u32[]{:S(2)}, u32[]{:S(2)}) collective-permute-start(f32[24,128]{1,0:T(8,128)S(1)} %get-tuple-element.13), channel_id=1, source_target_pairs={{1,2},{3,4},{5,6},{2,1},{4,3},{6,5},{9,10},{11,12},{13,14},{10,9},... | collective-permute-start | bytes 36872 | tf_op jit(solution)/shard_map/ppermute | solution.py:260
  33.4 21.1 %collective-permute-start.2 = (f32[24,256]{1,0:T(8,128)S(1)}, f32[24,256]{1,0:T(8,128)S(1)}, u32[]{:S(2)}, u32[]{:S(2)}) collective-permute-start(f32[24,256]{1,0:T(8,128)S(1)} %get-tuple-element.16.with_ref), channel_id=1, source_target_pairs={{0,8},{16,24},{32,40},{48,56},{64,72},{80,88},{96,104},{112,120},{... | collective-permute-start | bytes 73736 | tf_op jit(solution)/shard_map/ppermute | solution.py:260
  34.8 19.6 %collective-permute-start.3 = (f32[24,256]{1,0:T(8,128)S(1)}, f32[24,256]{1,0:T(8,128)S(1)}, u32[]{:S(2)}, u32[]{:S(2)}) collective-permute-start(f32[24,256]{1,0:T(8,128)S(1)} %get-tuple-element.17.off_ref), channel_id=1, source_target_pairs={{8,16},{24,32},{40,48},{56,64},{72,80},{88,96},{104,112},{16,8},{3... | collective-permute-start | bytes 73736 | tf_op jit(solution)/shard_map/ppermute | solution.py:260
  38.6 15.8 %copy-start.6 = (f32[2]{0:T(128)S(1)}, f32[2]{0:T(128)}, u32[]{:S(2)}) copy-start(f32[2]{0:T(128)} %lw_ref.1) | copy-start | bytes 28
